TPU v7x, 32 devices: a whole 2x2x4 slice. The times are simulated.
32 devices in a mesh: expert: 8 (over z, y), seq: 4 (over x, core).
Axes of the slice: x: 2, y: 2, z: 4, core: 2. Of those that a mesh axis runs over, the one named last changes fastest.
Arguments:
- inputs: bfloat16 [16, 1024, 1024], P('expert', 'seq'), may hold values from -6 to 6
- query_key_value_weight: bfloat16 [1024, 3072], replicated, may hold values from -0.25 to 0.25
- output_weight: bfloat16 [1024, 1024], replicated, may hold values from -1.5 to 1.5
- gain_attn: float32 [1024], replicated, may hold values from 0.25 to 1.75
- gain_ffn: float32 [1024], replicated, may hold values from 0.25 to 1.75
- w_up: bfloat16 [8, 4096, 1024], P('expert', 'seq'), may hold values from -0.1875 to 0.1875
- w_down: bfloat16 [8, 4096, 1024], P('expert', 'seq'), may hold values from -0.1875 to 0.1875
- expert_of: int32 [16, 1024], P('expert', 'seq'), may hold values from 0 to 7, as said below
- cotangent: bfloat16 [16, 1024, 1024], P('expert', 'seq'), may hold values from -6 to 6
Outputs:
- block_out: bfloat16 [16, 1024, 1024], P('expert', 'seq')
- input_grad: float32 [16, 1024, 1024], P('expert', 'seq')
- qkv_grad: float32 [1024, 3072], replicated
- out_grad: float32 [1024, 1024], replicated
- attn_gain_grad: float32 [1024], replicated
- ffn_gain_grad: float32 [1024], replicated
- up_grad: float32 [8, 4096, 1024], P('expert', 'seq')
- down_grad: float32 [8, 4096, 1024], P('expert', 'seq')
Inputs may be any that keep to these rules, and one draw needn't show every extreme that they name: `expert_of`: in every draw at most 128 tokens of one device (one index of each axis) name the same expert, and one expert is named by exactly 128 tokens of every device.
All inputs are finite; a program needn't handle non-finite values.
Results may differ from a plain program's by a relative error of at most 0.013.
The roundings to bfloat16 on the way count: a program that leaves them out, or rounds other values in their place, can miss the bound.
Values may be sent and summed in bfloat16 or wider, within the bound.
No kernel may reach another device: no remote copies, remote signals or barrier semaphores. Data moves between devices by JAX's collectives and lax.ppermute only.
A program may use at most 320 MiB of HBM per device.

v0:
```python
import jax
import jax.numpy as jnp
from jax import lax
from jax.sharding import PartitionSpec as P

HEAD_DIM = 64


epsilon = 1e-06


def rms_norm(values, scale_gain):
    inverse = lax.rsqrt(jnp.mean(values * values, axis=-1, keepdims=True) + epsilon)
    return values * inverse * scale_gain


def gelu_exact(values):
    return jax.nn.gelu(values, approximate=False)


def to_experts(slots_in):
    return lax.all_to_all(slots_in, "expert", split_axis=0, concat_axis=0, tiled=True)


def from_experts(slots_in):
    return lax.all_to_all(slots_in, "expert", split_axis=0, concat_axis=0, tiled=True)


def contract_first(left_side, right_side):
    return lax.dot_general(
        left_side, right_side, (((0,), (0,)), ((), ())), preferred_element_type=jnp.float32
    )


def contract_last(left_side, right_side):
    return lax.dot_general(
        left_side, right_side, (((1,), (1,)), ((), ())), preferred_element_type=jnp.float32
    )


def probabilities(queries, key_rows, first_place):
    scores = (
        jnp.einsum("sqhd,skhd->shqk", queries, key_rows, preferred_element_type=jnp.float32) * 0.125
    )
    query_place = first_place + jnp.arange(queries.shape[1], dtype=jnp.int32)
    key_place = jnp.arange(key_rows.shape[1], dtype=jnp.int32)
    causal = query_place[:, None] >= key_place[None, :]
    scores = jnp.where(causal[None, None, :, :], scores, -1e30)
    row_max = jnp.max(scores, axis=-1, keepdims=True)
    raised = jnp.exp(scores - row_max)
    return raised / jnp.sum(raised, axis=-1, keepdims=True)


def expert_forward(received, full_weights):
    full_up, full_down = full_weights
    pre_act = contract_last(received, full_up[0])
    activated = gelu_exact(pre_act).astype(jnp.bfloat16)
    result = jnp.dot(activated, full_down[0], preferred_element_type=jnp.float32).astype(
        jnp.bfloat16
    )
    return (result, (received, pre_act))


def expert_backward(grad_rows, expert_state, full_weights):
    rows_in, pre_act = expert_state
    activated, gelu_back = jax.vjp(gelu_exact, pre_act)
    act_low = activated.astype(jnp.bfloat16)
    full_up, full_down = full_weights
    grad_act = contract_last(grad_rows, full_down[0])
    grad_pre = gelu_back(grad_act)[0].astype(jnp.bfloat16)
    down_full = contract_first(act_low, grad_rows)
    up_full = contract_first(grad_pre, rows_in)
    grad_rows_in = jnp.dot(grad_pre, full_up[0], preferred_element_type=jnp.float32).astype(
        jnp.bfloat16
    )
    up_grad, down_grad = (
        lax.psum_scatter(up_full, "seq", scatter_dimension=0, tiled=True),
        lax.psum_scatter(down_full, "seq", scatter_dimension=0, tiled=True),
    )
    return (grad_rows_in, up_grad[None], down_grad[None])


def forward(
    inputs,
    query_key_value_weight,
    output_weight,
    gain_attn,
    gain_ffn,
    full_weights,
    slot_index,
    first_place,
    capacity,
):
    seq_count, local_len, model_width = inputs.shape
    head_count = model_width // HEAD_DIM
    token_rows = seq_count * local_len
    groups = lax.axis_size("expert")
    flat_in = inputs.reshape(token_rows, model_width).astype(jnp.float32)
    normed_input = rms_norm(flat_in, gain_attn).astype(jnp.bfloat16)
    projected_output = jnp.dot(
        normed_input, query_key_value_weight, preferred_element_type=jnp.float32
    ).astype(jnp.bfloat16)
    projected_output = projected_output.reshape(seq_count, local_len, 3, head_count, HEAD_DIM)
    queries = projected_output[:, :, 0]
    key_rows, value_rows = (
        lax.all_gather(projected_output[:, :, 1], "seq", axis=1, tiled=True),
        lax.all_gather(projected_output[:, :, 2], "seq", axis=1, tiled=True),
    )
    weights = probabilities(queries, key_rows, first_place).astype(jnp.bfloat16)
    attention_result = jnp.einsum(
        "shqk,skhd->sqhd", weights, value_rows, preferred_element_type=jnp.float32
    )
    attention_result = attention_result.astype(jnp.bfloat16).reshape(token_rows, model_width)
    hidden_state = flat_in + jnp.dot(
        attention_result, output_weight, preferred_element_type=jnp.float32
    )
    ffn_input = rms_norm(hidden_state, gain_ffn).astype(jnp.bfloat16)
    sending = (
        jnp.zeros((groups * capacity, model_width), jnp.bfloat16).at[slot_index].set(ffn_input)
    )
    received = to_experts(sending.reshape(groups, capacity, model_width)).reshape(
        groups * capacity, model_width
    )
    expert_out, expert_state = expert_forward(received, full_weights)
    returned = from_experts(expert_out.reshape(groups, capacity, model_width)).reshape(
        groups * capacity, model_width
    )
    block_out = hidden_state + returned[slot_index].astype(jnp.float32)
    kept_state = (
        flat_in,
        normed_input,
        queries,
        key_rows,
        value_rows,
        attention_result,
        hidden_state,
        expert_state,
    )
    return (block_out, kept_state)


def backward(
    kept_state,
    cotangent,
    query_key_value_weight,
    output_weight,
    gain_attn,
    gain_ffn,
    full_weights,
    slot_index,
    first_place,
    capacity,
):
    (
        flat_in,
        normed_input,
        queries,
        key_rows,
        value_rows,
        attention_result,
        hidden_state,
        expert_state,
    ) = kept_state
    token_rows, model_width = flat_in.shape
    groups = lax.axis_size("expert")
    grad_output = cotangent.reshape(token_rows, model_width)
    sending = (
        jnp.zeros((groups * capacity, model_width), jnp.bfloat16).at[slot_index].set(grad_output)
    )
    grad_expert = to_experts(sending.reshape(groups, capacity, model_width)).reshape(
        groups * capacity, model_width
    )
    grad_rows_in, up_grad, down_grad = expert_backward(grad_expert, expert_state, full_weights)
    grad_back = from_experts(grad_rows_in.reshape(groups, capacity, model_width)).reshape(
        groups * capacity, model_width
    )
    grad_ffn_input = grad_back[slot_index].astype(jnp.float32)
    unused, ffn_pull = jax.vjp(rms_norm, hidden_state, gain_ffn)
    grad_hidden_norm, ffn_gain_grad = ffn_pull(grad_ffn_input)
    grad_hidden = grad_output.astype(jnp.float32) + grad_hidden_norm
    grad_branch = grad_hidden.astype(jnp.bfloat16)
    out_grad = contract_first(attention_result, grad_branch)
    grad_attended = (
        contract_last(grad_branch, output_weight).astype(jnp.bfloat16).reshape(queries.shape)
    )
    weights = probabilities(queries, key_rows, first_place)
    weights_low = weights.astype(jnp.bfloat16)
    grad_weights = jnp.einsum(
        "sqhd,skhd->shqk", grad_attended, value_rows, preferred_element_type=jnp.float32
    )
    row_total = jnp.sum(grad_weights * weights, axis=-1, keepdims=True)
    grad_scores = (weights * (grad_weights - row_total)).astype(jnp.bfloat16)
    grad_queries = 0.125 * jnp.einsum(
        "shqk,skhd->sqhd", grad_scores, key_rows, preferred_element_type=jnp.float32
    )
    grad_keys = 0.125 * jnp.einsum(
        "shqk,sqhd->skhd", grad_scores, queries, preferred_element_type=jnp.float32
    )
    grad_values = jnp.einsum(
        "shqk,sqhd->skhd", weights_low, grad_attended, preferred_element_type=jnp.float32
    )
    grad_keys, grad_values = (
        lax.psum_scatter(grad_keys, "seq", scatter_dimension=1, tiled=True),
        lax.psum_scatter(grad_values, "seq", scatter_dimension=1, tiled=True),
    )
    grad_projected = jnp.stack((grad_queries, grad_keys, grad_values), axis=2).astype(jnp.bfloat16)
    grad_projected = grad_projected.reshape(token_rows, 3 * model_width)
    qkv_grad = contract_first(normed_input, grad_projected)
    grad_normed = contract_last(grad_projected, query_key_value_weight)
    unused_again, input_pull = jax.vjp(rms_norm, flat_in, gain_attn)
    grad_input_norm, attn_gain_grad = input_pull(grad_normed)
    input_grad = grad_hidden + grad_input_norm
    qkv_grad, out_grad, attn_gain_grad, ffn_gain_grad = lax.psum(
        (qkv_grad, out_grad, attn_gain_grad, ffn_gain_grad), ("expert", "seq")
    )
    return (input_grad, qkv_grad, out_grad, attn_gain_grad, ffn_gain_grad, up_grad, down_grad)


def shards(
    inputs,
    query_key_value_weight,
    output_weight,
    gain_attn,
    gain_ffn,
    w_up,
    w_down,
    expert_of,
    cotangent,
):
    groups = lax.axis_size("expert")
    seq_count, local_len, model_width = inputs.shape
    token_rows = seq_count * local_len
    capacity = max(2, 2 * token_rows // groups)
    routes = expert_of.reshape(token_rows)
    one_hot = (routes[:, None] == jnp.arange(groups, dtype=jnp.int32)[None, :]).astype(jnp.int32)
    position = jnp.sum(jnp.cumsum(one_hot, axis=0) * one_hot, axis=1) - 1
    slot_index = routes * capacity + position
    first_place = lax.axis_index("seq") * local_len
    full_weights = (
        lax.all_gather(w_up, "seq", axis=1, tiled=True),
        lax.all_gather(w_down, "seq", axis=1, tiled=True),
    )
    block_out, dropped = forward(
        inputs,
        query_key_value_weight,
        output_weight,
        gain_attn,
        gain_ffn,
        full_weights,
        slot_index,
        first_place,
        capacity,
    )
    barrier_out = lax.optimization_barrier((inputs, block_out))
    unused, kept_state = forward(
        barrier_out[0],
        query_key_value_weight,
        output_weight,
        gain_attn,
        gain_ffn,
        full_weights,
        slot_index,
        first_place,
        capacity,
    )
    results = backward(
        kept_state,
        cotangent,
        query_key_value_weight,
        output_weight,
        gain_attn,
        gain_ffn,
        full_weights,
        slot_index,
        first_place,
        capacity,
    )
    input_grad, qkv_grad, out_grad, attn_gain_grad, ffn_gain_grad, up_grad, down_grad = results
    return (
        block_out.astype(jnp.bfloat16).reshape(inputs.shape),
        input_grad.reshape(inputs.shape),
        qkv_grad,
        out_grad,
        attn_gain_grad,
        ffn_gain_grad,
        up_grad,
        down_grad,
    )


def solution(mesh):
    in_specs = (
        P("expert", "seq", None),
        P(),
        P(),
        P(),
        P(),
        P("expert", "seq", None),
        P("expert", "seq", None),
        P("expert", "seq"),
        P("expert", "seq", None),
    )
    out_specs = (
        P("expert", "seq", None),
        P("expert", "seq", None),
        P(),
        P(),
        P(),
        P(),
        P("expert", "seq", None),
        P("expert", "seq", None),
    )
    return jax.shard_map(shards, mesh=mesh, in_specs=in_specs, out_specs=out_specs, check_vma=False)
```

profile of v0, /device:TPU:0, one launch (start us, length us, event | category | flops | bytes accessed | tf_op | source)
XLA Modules:
  0.0 1428.0 jit_solution(2788046305029156179)
XLA Ops:
  10.4 7.5 convolution_convert_fusion.1
  18.0 8.5 reshape.313
  26.5 6.0 fusion.165
  32.5 3.5 copy.47
  36.2 3.6 copy.45
  42.3 2.9 copy.46
  45.2 28.8 %all-gather.17.cloned.1.call-done = bf16[2,1024,1,16,64]{1,4,3,0,2:T(8,128)(2,1)} async-done(((bf16[2,256,1,16,64]{1,4,3,0,2:T(8,128)(2,1)}), bf16[2,1024,1,16,64]{1,4,3,0,2:T(8,128)(2,1)}) %all-gather.17.cloned.1.call-update) | async-done | bytes 4194320 | tf_op jit(solution)/shard_map/all_gather | solution.py:106
  74.0 16.6 %fusion.57 = f32[2,16,256,1024]{3,2,1,0:T(8,128)} fusion(bf16[2,1024,1,16,64]{1,4,3,0,2:T(8,128)(2,1)} %all-gather.17.cloned.1.call-done, bf16[2,256,1,16,64]{1,4,3,0,2:T(8,128)(2,1)S(1)} %copy.46), kind=kOutput, calls=%fused_computation.87 | convolution fusion | flops 1073741824 | bytes 38797312 | tf_op jit(solution)/shard_map/sqhd,skhd->shqk/dot_general | solution.py:43
  90.6 40.6 %fusion.166 = (f32[2,16,256]{2,1,0:T(8,128)S(1)}, f32[2,16,256,1024]{3,2,1,0:T(8,128)}) fusion(f32[2,16,256,1024]{3,2,1,0:T(8,128)} %fusion.57, pred[256,1024]{1,0:T(8,128)(4,1)S(1)} %iota_compare_fusion), kind=kOutput, calls=%fused_computation.208 | output fusion | flops 50332672 | bytes 67403776 | tf_op jit(solution)/shard_map/sub | solution.py:50
  131.1 16.4 %fusion.100 = bf16[2,256,16,64]{1,3,2,0:T(8,128)(2,1)} fusion(f32[2,16,256,1024]{3,2,1,0:T(8,128)} %get-tuple-element.27, f32[2,16,256]{2,1,0:T(8,128)S(1)} %get-tuple-element.26, bf16[2,1024,1,16,64]{1,4,3,0,2:T(8,128)(2,1)} %all-gather.15.cloned.1.call-done), kind=kOutput, calls=%fused_computation.132 | convolution fusion | flops 1091043328 | bytes 38830080 | tf_op jit(solution)/shard_map/shqk,skhd->sqhd/dot_general | solution.py:110
  147.5 2.4 copy.29
  150.2 2.6 multiply_reduce_fusion.2
  152.8 5.3 scatter_custom_fusion
  158.1 5.0 all-to-all-start
  163.7 48.2 %all-to-all-done = bf16[8,128,1024]{2,1,0:T(8,128)(2,1)} async-done(((bf16[8,128,1024]{2,1,0:T(8,128)(2,1)}), bf16[8,128,1024]{2,1,0:T(8,128)(2,1)}, u32[]{:S(2)}, u32[]{:S(2)}) %all-to-all-start) | async-done | bytes 2097184 | tf_op jit(solution)/shard_map/all_to_all | solution.py:22
  211.9 47.1 %fusion.204 = bf16[1024,4096]{1,0:T(8,128)(2,1)} fusion(bf16[1024,1024]{1,0:T(8,128)(2,1)} %bitcast.10, bf16[1,4096,1024]{2,1,0:T(8,128)(2,1)} %all-gather.11.cloned.1.call-done), kind=kOutput, calls=%fused_computation.20.clone.clone.clone.clone.1 | convolution fusion | flops 8862564352 | bytes 18874368 | tf_op jit(solution)/shard_map/dot_general | solution.py:36
  259.0 14.6 %fusion.83 = bf16[1024,1024]{1,0:T(8,128)(2,1)} fusion(bf16[1,4096,1024]{2,1,0:T(8,128)(2,1)} %all-gather.13.cloned.1.call-done, bf16[1024,4096]{1,0:T(8,128)(2,1)} %fusion.204), kind=kOutput, calls=%fused_computation.128 | convolution fusion | flops 8590983168 | bytes 18874368 | tf_op jit(solution)/shard_map/dot_general | solution.py:58
  273.7 4.5 all-to-all-start.1
  278.2 47.7 %all-to-all-done.1 = bf16[8,128,1024]{2,1,0:T(8,128)(2,1)} async-done(((bf16[8,128,1024]{2,1,0:T(8,128)(2,1)}), bf16[8,128,1024]{2,1,0:T(8,128)(2,1)}, u32[]{:S(2)}, u32[]{:S(2)}) %all-to-all-start.1) | async-done | bytes 2097184 | tf_op jit(solution)/shard_map/all_to_all | solution.py:26
  325.9 5.8 gather_fusion
  331.7 3.2 convert_add_fusion
  337.2 7.6 convolution_convert_fusion
  344.8 8.5 reshape.314
  353.3 6.0 fusion.164
  359.3 3.5 copy.50
  363.0 3.7 copy.48
  366.7 3.6 copy.49
  370.4 25.9 %all-gather.21.cloned.1.call-done = bf16[2,1024,1,16,64]{1,4,3,0,2:T(8,128)(2,1)} async-done(((bf16[2,256,1,16,64]{1,4,3,0,2:T(8,128)(2,1)}), bf16[2,1024,1,16,64]{1,4,3,0,2:T(8,128)(2,1)}) %all-gather.21.cloned.1.call-update) | async-done | bytes 4194320 | tf_op jit(solution)/shard_map/all_gather | solution.py:106
  396.2 19.5 %fusion.52 = f32[2,16,256,1024]{3,2,1,0:T(8,128)} fusion(bf16[2,1024,1,16,64]{1,4,3,0,2:T(8,128)(2,1)} %all-gather.21.cloned.1.call-done, bf16[2,256,1,16,64]{1,4,3,0,2:T(8,128)(2,1)} %copy.49), kind=kOutput, calls=%fused_computation.82 | convolution fusion | flops 1073741824 | bytes 38797312 | tf_op jit(solution)/shard_map/sqhd,skhd->shqk/dot_general | solution.py:43
  415.7 37.5 %fusion.167 = (f32[2,16,256]{2,1,0:T(8,128)S(1)}, f32[2,16,256,1024]{3,2,1,0:T(8,128)}) fusion(f32[2,16,256,1024]{3,2,1,0:T(8,128)} %fusion.52, pred[256,1024]{1,0:T(8,128)(4,1)S(1)} %copy-done.10), kind=kOutput, calls=%fused_computation.209 | output fusion | flops 50332672 | bytes 67403776 | tf_op jit(solution)/shard_map/sub | solution.py:50
  453.2 16.2 %fusion.103 = bf16[2,256,16,64]{1,3,2,0:T(8,128)(2,1)} fusion(bf16[2,1024,1,16,64]{1,4,3,0,2:T(8,128)(2,1)} %all-gather.19.cloned.1.call-done, f32[2,16,256,1024]{3,2,1,0:T(8,128)} %get-tuple-element.31, f32[2,16,256]{2,1,0:T(8,128)S(1)} %get-tuple-element.30), kind=kOutput, calls=%fused_computation.133 | convolution fusion | flops 1091043328 | bytes 38830080 | tf_op jit(solution)/shard_map/shqk,skhd->sqhd/dot_general | solution.py:110
  471.9 2.6 multiply_reduce_fusion.1
  475.2 5.3 scatter_custom_fusion.1
  480.4 5.6 all-to-all-start.2
  486.0 4.8 scatter_custom_fusion.2
  490.8 44.0 %all-to-all-done.2 = bf16[8,128,1024]{2,1,0:T(8,128)(2,1)} async-done(((bf16[8,128,1024]{2,1,0:T(8,128)(2,1)}), bf16[8,128,1024]{2,1,0:T(8,128)(2,1)}, u32[]{:S(2)}, u32[]{:S(2)}) %all-to-all-start.2) | async-done | bytes 2097184 | tf_op jit(solution)/shard_map/all_to_all | solution.py:22
  534.8 4.3 all-to-all-start.3
  539.2 46.6 %fusion.7 = (f32[1024,4096]{1,0:T(8,128)}, f32[1024,4096]{1,0:T(8,128)}) fusion(bf16[1024,1024]{1,0:T(8,128)(2,1)} %bitcast.23, bf16[1,4096,1024]{2,1,0:T(8,128)(2,1)} %all-gather.11.cloned.1.call-done), kind=kOutput, calls=%fused_computation.21 | convolution fusion | flops 8849981440 | bytes 44040192 | tf_op jit(solution)/shard_map/dot_general | solution.py:36
  586.9 23.2 %add_convert_fusion = bf16[1024,4096]{1,0:T(8,128)(2,1)} fusion(f32[1024,4096]{1,0:T(8,128)} %get-tuple-element.34, f32[1024,4096]{1,0:T(8,128)} %get-tuple-element.35, bf16[1024,1024]{1,0:T(8,128)(2,1)} %bitcast.25, bf16[1,4096,1024]{2,1,0:T(8,128)(2,1)} %all-gather.13.cloned.1.call-done), kind=kOutput, calls=%fused_computation.23 | convolution fusion | flops 8648654848 | bytes 52428800 | tf_op jit(solution)/shard_map/dot_general | solution.py:36
  610.2 13.8 fusion.80
  624.0 52.1 %all_to_all.25 = bf16[8,128,1024]{2,1,0:T(8,128)(2,1)} all-to-all(bf16[8,128,1024]{2,1,0:T(8,128)(2,1)S(1)} %bitcast.202), channel_id=1, replica_groups=mesh['expert'=8,'seq'=4] {'expert'}, dimensions={0} | all-to-all | bytes 4194304 | tf_op jit(solution)/shard_map/all_to_all | solution.py:26
  676.1 4.6 gather_fusion.1
  680.7 2.9 fusion.66
  683.6 2.4 fusion.67
  691.0 2.8 copy.36
  693.8 16.0 %fusion.60 = f32[2,1024,16,64]{1,3,2,0:T(8,128)} fusion(bf16[2,256,16,64]{1,3,2,0:T(8,128)(2,1)S(1)} %copy.36, f32[2,16,256,1024]{3,2,1,0:T(8,128)} %get-tuple-element.31, f32[2,16,256]{2,1,0:T(8,128)S(1)} %copy-done.17), kind=kOutput, calls=%fused_computation.90 | convolution fusion | flops 1090519040 | bytes 43024384 | tf_op jit(solution)/shard_map/shqk,sqhd->skhd/dot_general | solution.py:199
  709.9 25.3 %multiply_reduce_fusion = (f32[2,16,256]{2,1,0:T(8,128)S(1)}, f32[2,16,256,1024]{3,2,1,0:T(8,128)}) fusion(f32[2,16,256,1024]{3,2,1,0:T(8,128)} %get-tuple-element.31, f32[2,16,256]{2,1,0:T(8,128)S(1)} %copy-done.17, bf16[2,256,16,64]{1,3,2,0:T(8,128)(2,1)S(1)} %copy.36, bf16[2,1024,1,16,64]{1,4,3,0,2:T(8,128)(2,1)} %all-gather.19.cloned.1.call-done), kind=kOutput, calls=%fused_computation.8 | convolution fusion | flops 1098899456 | bytes 72417280 | tf_op jit(solution)/shard_map/sqhd,skhd->shqk/dot_general | solution.py:188
  735.3 28.4 %multiply_convert_fusion = bf16[2,16,256,1024]{3,2,1,0:T(8,128)(2,1)} fusion(f32[2,16,256,1024]{3,2,1,0:T(8,128)} %get-tuple-element.37, f32[2,16,256]{2,1,0:T(8,128)S(1)} %get-tuple-element.36, f32[2,16,256,1024]{3,2,1,0:T(8,128)} %get-tuple-element.31, f32[2,16,256]{2,1,0:T(8,128)S(1)} %copy-done.17), kind=kLoop, calls=%fused_computation.7 | loop fusion | flops 33554432 | bytes 83951616 | tf_op jit(solution)/shard_map/convert_element_type | solution.py:192
  763.7 12.5 multiply_bitcast_fusion
  777.9 5.2 fusion.121
  783.1 14.4 %multiply_bitcast_fusion.1 = bf16[2,256,1,16,64]{1,4,3,0,2:T(8,128)(2,1)} fusion(bf16[2,16,256,1024]{3,2,1,0:T(8,128)(2,1)} %multiply_convert_fusion, bf16[2,1024,1,16,64]{1,4,3,0,2:T(8,128)(2,1)} %all-gather.21.cloned.1.call-done), kind=kOutput, calls=%fused_computation.121 | convolution fusion | flops 1074790400 | bytes 22020096 | tf_op jit(solution)/shard_map/shqk,skhd->sqhd/dot_general | solution.py:193
  797.5 56.7 %reduce-scatter.5.cloned.1.call-done = f32[2,256,16,64]{1,3,2,0:T(8,128)} async-done(((f32[2,1024,16,64]{1,3,2,0:T(8,128)}), f32[2,256,16,64]{1,3,2,0:T(8,128)}) %reduce-scatter.5.cloned.1.call-update) | async-done | bytes 2097168 | tf_op jit(solution)/shard_map/reduce_scatter | solution.py:203
  854.3 3.2 maximum_convert_fusion
  857.4 3.3 copy.38
  863.0 6.6 fusion.168
  869.9 25.9 %fusion.27 = f32[4096,1024]{1,0:T(8,128)} fusion(bf16[1024,1024]{1,0:T(8,128)(2,1)} %bitcast.25, f32[1024,4096]{1,0:T(8,128)} %get-tuple-element.34, f32[1024,4096]{1,0:T(8,128)} %get-tuple-element.35), kind=kOutput, calls=%fused_computation.60 | convolution fusion | flops 8602517504 | bytes 52428800 | tf_op jit(solution)/shard_map/dot_general | solution.py:30
  895.9 16.3 %fusion.169 = f32[4096,1024]{1,0:T(8,128)} fusion(bf16[1024,4096]{1,0:T(8,128)(2,1)} %add_convert_fusion, bf16[1024,1024]{1,0:T(8,128)(2,1)} %bitcast.23), kind=kOutput, calls=%fused_computation.211 | convolution fusion | flops 8589934592 | bytes 27262976 | tf_op jit(solution)/shard_map/dot_general | solution.py:30
  912.9 9.4 fusion.72
  922.4 40.8 %all-reduce = (f32[1024]{0:T(1024)}, f32[1024]{0:T(1024)}) all-reduce(f32[1024]{0:T(1024)S(1)} %get-tuple-element.12, f32[1024]{0:T(1024)S(1)} %copy-done.27), channel_id=1, replica_groups=mesh['expert'=8,'seq'=4] {'expert','seq'}, use_global_device_ids=true, to_apply=%region_22.23 | all-reduce | flops 2048 | bytes 16384 | tf_op jit(solution)/shard_map/psum | solution.py:213
  963.2 4.8 fusion.68
  968.0 181.6 %all-reduce.4.cloned.1.call-done = (f32[1024,3072]{1,0:T(8,128)}, f32[1024,1024]{1,0:T(8,128)}) async-done(((f32[1024,3072]{1,0:T(8,128)}, f32[1024,1024]{1,0:T(8,128)}), (f32[1024,3072]{1,0:T(8,128)}, f32[1024,1024]{1,0:T(8,128)})) %all-reduce.4.cloned.1.call-update) | async-done | bytes 16777232 | tf_op jit(solution)/shard_map/psum | solution.py:213
  1149.6 129.0 %reduce-scatter.11.cloned.1.call-done = f32[1024,1024]{1,0:T(8,128)} async-done(((f32[4096,1024]{1,0:T(8,128)}), f32[1024,1024]{1,0:T(8,128)}) %reduce-scatter.11.cloned.1.call-update) | async-done | bytes 4194320 | tf_op jit(solution)/shard_map/reduce_scatter | solution.py:78
  1278.6 129.5 %reduce-scatter.9.cloned.1.call-done = f32[1024,1024]{1,0:T(8,128)} async-done(((f32[4096,1024]{1,0:T(8,128)}), f32[1024,1024]{1,0:T(8,128)}) %reduce-scatter.9.cloned.1.call-update) | async-done | bytes 4194320 | tf_op jit(solution)/shard_map/reduce_scatter | solution.py:77
  1408.1 11.1 copy.60
  (130 shorter events, 25.6 us)
Async XLA Ops:
  7.2 143.0 %copy-start = (bf16[1024,1024]{1,0:T(8,128)(2,1)S(1)}, bf16[1024,1024]{1,0:T(8,128)(2,1)}, u32[]{:S(2)}) copy-start(bf16[1024,1024]{1,0:T(8,128)(2,1)} %param.11) | copy-start | bytes 6291460
  7.2 66.8 %all-gather.17.cloned.1.call-start = ((), (), s32[]{:S(2)}) async-start(), calls=%async_computation.16 | async-start | bytes 5242880 | tf_op jit(solution)/shard_map/all_gather | solution.py:106
  26.5 14.0 copy-start.26
  36.1 95.0 %all-gather.15.cloned.1.call-start = ((), (), s32[]{:S(2)}) async-start(), calls=%async_computation.15 | async-start | bytes 5242880 | tf_op jit(solution)/shard_map/all_gather | solution.py:107
  39.7 172.2 %all-gather.11.cloned.1.call-start = ((), (), s32[]{:S(2)}) async-start(), calls=%async_computation.9 | async-start | bytes 10485760 | tf_op jit(solution)/shard_map/all_gather | solution.py:240
  42.3 48.3 %copy-start.9 = (pred[256,1024]{1,0:T(8,128)(4,1)}, pred[256,1024]{1,0:T(8,128)(4,1)S(1)}, u32[]{:S(2)}) copy-start(pred[256,1024]{1,0:T(8,128)(4,1)S(1)} %iota_compare_fusion) | copy-start | bytes 786436
  45.2 107.6 %copy-start.31 = (s32[512,1]{0,1:T(1,128)}, s32[512,1]{0,1:T(1,128)S(1)}, u32[]{:S(2)}) copy-start(s32[512,1]{0,1:T(1,128)S(1)} %compare_select_fusion) | copy-start | bytes 6148
  131.1 19.0 %copy-start.1 = (bf16[2,256,1024]{2,1,0:T(8,128)(2,1)S(1)}, bf16[2,256,1024]{2,1,0:T(8,128)(2,1)}, u32[]{:S(2)}) copy-start(bf16[2,256,1024]{2,1,0:T(8,128)(2,1)} %param.9) | copy-start | bytes 3145732
  131.1 21.7 %copy-start.11 = (f32[1024]{0:T(1024)S(1)}, f32[1024]{0:T(1024)}, u32[]{:S(2)}) copy-start(f32[1024]{0:T(1024)} %param.13) | copy-start | bytes 12292
  158.1 53.8 %all-to-all-start = ((bf16[8,128,1024]{2,1,0:T(8,128)(2,1)}), bf16[8,128,1024]{2,1,0:T(8,128)(2,1)}, u32[]{:S(2)}, u32[]{:S(2)}) async-start(bf16[8,128,1024]{2,1,0:T(8,128)(2,1)} %bitcast.193), calls=%async_computation | async-start | bytes 4194304 | tf_op jit(solution)/shard_map/all_to_all | solution.py:22
  163.1 95.9 %all-gather.13.cloned.1.call-start = ((), (), s32[]{:S(2)}) async-start(), calls=%async_computation.10 | async-start | bytes 10485760 | tf_op jit(solution)/shard_map/all_gather | solution.py:241
  259.0 19.2 %copy-start.32 = (s32[512,1]{0,1:T(1,128)S(1)}, s32[512,1]{0,1:T(1,128)}, u32[]{:S(2)}) copy-start(s32[512,1]{0,1:T(1,128)} %copy-done.31) | copy-start | bytes 6148
  273.7 61.2 %copy-start.2 = (bf16[2,256,1024]{2,1,0:T(8,128)(2,1)S(1)}, bf16[2,256,1024]{2,1,0:T(8,128)(2,1)}, u32[]{:S(2)}) copy-start(bf16[2,256,1024]{2,1,0:T(8,128)(2,1)} %param.9) | copy-start | bytes 3145732
  273.7 63.3 %copy-start.14 = (f32[1024]{0:T(1024)S(1)}, f32[1024]{0:T(1024)}, u32[]{:S(2)}) copy-start(f32[1024]{0:T(1024)} %param.12) | copy-start | bytes 12292
  273.7 52.2 %all-to-all-start.1 = ((bf16[8,128,1024]{2,1,0:T(8,128)(2,1)}), bf16[8,128,1024]{2,1,0:T(8,128)(2,1)}, u32[]{:S(2)}, u32[]{:S(2)}) async-start(bf16[8,128,1024]{2,1,0:T(8,128)(2,1)} %bitcast.201), calls=%async_computation.1 | async-start | bytes 4194304 | tf_op jit(solution)/shard_map/all_to_all | solution.py:26
  278.1 118.1 %all-gather.21.cloned.1.call-start = ((), (), s32[]{:S(2)}) async-start(), calls=%async_computation.18 | async-start | bytes 5242880 | tf_op jit(solution)/shard_map/all_gather | solution.py:106
  278.2 66.6 %copy-start.28 = (s32[1024]{0:T(1024)}, s32[1024]{0:T(1024)S(1)}, u32[]{:S(2)}) copy-start(s32[1024]{0:T(1024)S(1)} %pad_clamp_fusion) | copy-start | bytes 12292
  335.7 0.6 copy-start.24
  336.3 0.6 copy-start.20
  362.9 90.3 %all-gather.19.cloned.1.call-start = ((), (), s32[]{:S(2)}) async-start(), calls=%async_computation.17 | async-start | bytes 5242880 | tf_op jit(solution)/shard_map/all_gather | solution.py:107
  370.4 45.3 %copy-start.10 = (pred[256,1024]{1,0:T(8,128)(4,1)S(1)}, pred[256,1024]{1,0:T(8,128)(4,1)}, u32[]{:S(2)}) copy-start(pred[256,1024]{1,0:T(8,128)(4,1)} %copy-done.9) | copy-start | bytes 786436
  453.2 16.2 %copy-start.16 = (f32[2,16,256]{2,1,0:T(8,128)}, f32[2,16,256]{2,1,0:T(8,128)S(1)}, u32[]{:S(2)}) copy-start(f32[2,16,256]{2,1,0:T(8,128)S(1)} %get-tuple-element.30) | copy-start | bytes 98308
  453.2 22.0 %copy-start.12 = (f32[1024]{0:T(1024)S(1)}, f32[1024]{0:T(1024)}, u32[]{:S(2)}) copy-start(f32[1024]{0:T(1024)} %param.13) | copy-start | bytes 12292
  471.9 2.6 copy-start.5
  474.6 0.6 copy-start.22
  475.2 110.6 %copy-start.18 = (f32[512]{0:T(512)}, f32[512]{0:T(512)S(1)}, u32[]{:S(2)}) copy-start(f32[512]{0:T(512)S(1)} %fusion.126) | copy-start | bytes 6148
  480.4 54.3 %all-to-all-start.2 = ((bf16[8,128,1024]{2,1,0:T(8,128)(2,1)}), bf16[8,128,1024]{2,1,0:T(8,128)(2,1)}, u32[]{:S(2)}, u32[]{:S(2)}) async-start(bf16[8,128,1024]{2,1,0:T(8,128)(2,1)} %bitcast.194), calls=%async_computation.2 | async-start | bytes 4194304 | tf_op jit(solution)/shard_map/all_to_all | solution.py:22
  534.8 52.2 %all-to-all-start.3 = ((bf16[8,128,1024]{2,1,0:T(8,128)(2,1)}), bf16[8,128,1024]{2,1,0:T(8,128)(2,1)}, u32[]{:S(2)}, u32[]{:S(2)}) async-start(bf16[8,128,1024]{2,1,0:T(8,128)(2,1)} %bitcast.195), calls=%async_computation.3 | async-start | bytes 4194304 | tf_op jit(solution)/shard_map/all_to_all | solution.py:22
  539.1 258.4 %reduce-scatter.7.cloned.1.call-start = ((), (), s32[]{:S(2)}) async-start(), calls=%async_computation.12 | async-start | bytes 10485760 | tf_op jit(solution)/shard_map/reduce_scatter | solution.py:204
  610.2 65.9 %copy-start.29 = (s32[1024]{0:T(1024)S(1)}, s32[1024]{0:T(1024)}, u32[]{:S(2)}) copy-start(s32[1024]{0:T(1024)} %copy-done.28) | copy-start | bytes 12292
  624.0 56.7 %copy-start.13 = (f32[1024]{0:T(1024)S(1)}, f32[1024]{0:T(1024)}, u32[]{:S(2)}) copy-start(f32[1024]{0:T(1024)} %param.13) | copy-start | bytes 12292
  624.0 56.7 %copy-start.19 = (f32[512]{0:T(512)S(1)}, f32[512]{0:T(512)}, u32[]{:S(2)}) copy-start(f32[512]{0:T(512)} %copy-done.18) | copy-start | bytes 6148
  624.0 59.6 %copy-start.23 = (f32[512]{0:T(512)S(1)}, f32[512]{0:T(512)}, u32[]{:S(2)}) copy-start(f32[512]{0:T(512)} %copy-done.22) | copy-start | bytes 6148
  680.7 13.1 copy-start.17
  686.1 1.3 copy-start.4
  709.9 144.4 %reduce-scatter.5.cloned.1.call-start = ((), (), s32[]{:S(2)}) async-start(), calls=%async_computation.11 | async-start | bytes 10485760 | tf_op jit(solution)/shard_map/reduce_scatter | solution.py:203
  763.6 13.0 copy-start.3
  763.6 13.0 copy-start.15
  763.6 13.0 copy-start.30
  776.2 373.4 %all-reduce.4.cloned.1.call-start = ((), (), s32[]{:S(2)}) async-start(), calls=%async_computation.19 | async-start | bytes 33554432 | tf_op jit(solution)/shard_map/psum | solution.py:213
  854.2 8.8 copy-start.8
  861.4 1.6 copy-start.7
  869.7 408.9 %reduce-scatter.11.cloned.1.call-start = ((), (), s32[]{:S(2)}) async-start(), calls=%async_computation.14 | async-start | bytes 20971520 | tf_op jit(solution)/shard_map/reduce_scatter | solution.py:78
  895.9 512.2 %reduce-scatter.9.cloned.1.call-start = ((), (), s32[]{:S(2)}) async-start(), calls=%async_computation.13 | async-start | bytes 20971520 | tf_op jit(solution)/shard_map/reduce_scatter | solution.py:77
  912.2 0.7 copy-start.21
  912.9 9.5 copy-start.27
  912.9 50.3 %copy-start.25 = (f32[1,2,2,128]{3,1,2,0:T(2,128)S(1)}, f32[1,2,2,128]{3,1,2,0:T(2,128)}, u32[]{:S(2)}) copy-start(f32[1,2,2,128]{3,1,2,0:T(2,128)} %copy-done.24) | copy-start | bytes 6148
  1408.1 11.1 copy-start.6
Sparse Core Ops, SparseCore 0:
  36.2 37.7 all-gather.16
  76.1 35.0 all-gather.14
  112.7 58.2 all-gather.10
  172.5 58.2 all-gather.12
  363.0 33.1 all-gather.20
  398.2 35.0 all-gather.18
  710.0 69.7 reduce-scatter.6
  782.5 71.6 reduce-scatter.4
  869.8 279.7 all-reduce.3
  1152.6 125.9 reduce-scatter.10
  1281.9 126.1 reduce-scatter.8
where the time goes:
time: 1430 us
  waiting for transfers between devices  694 us (49%)
  matrix products  367 us (26%)
  other arithmetic  141 us (10%)
  local copies, waits for them, and re-layouts  98.3 us (7%)
  blocking collectives  92.9 us (6%)
  starting transfers between devices  20.6 us (1%)
  between operations  14.5 us (1%)
    psum x1, waiting for transfers between devices, backward(): lax.psum((qkv_grad, out_grad, attn_gain_grad, ffn_gain_grad), ('expert',...  182 us
    reduce_scatter x1, waiting for transfers between devices, expert_backward(): lax.psum_scatter(up_full, 'seq', scatter_dimension=0, tiled=True)  129 us
    reduce_scatter x1, waiting for transfers between devices, expert_backward(): lax.psum_scatter(down_full, 'seq', scatter_dimension=0, tiled=True)  129 us
    dot_general x5, matrix products, contract_last(): lax.dot_general(left_side, right_side, (((1,), (1,)), ((), ())), preferre...  128 us
    all_to_all x3, waiting for transfers between devices, to_experts(): lax.all_to_all(slots_in, 'expert', split_axis=0, concat_axis=0, tiled=True)  93.4 us
    sub x2, other arithmetic, probabilities(): raised = jnp.exp(scores - row_max)  78 us
    reduce_scatter x1, waiting for transfers between devices, backward(): lax.psum_scatter(grad_keys, 'seq', scatter_dimension=1, tiled=True)  56.7 us
    all_gather x2, waiting for transfers between devices, forward(): lax.all_gather(projected_output[:, :, 1], 'seq', axis=1, tiled=True)  54.6 us
  transfers between devices with their start and end apart: 15, of which 10 were waited for; matrix products, arithmetic and copies ran while one was open for 28% of the time, Pallas kernels for 0%

commit v1 on v0

v1 whole, which is shorter than its diff:
```python
import jax
import jax.numpy as jnp
from jax import lax
from jax.experimental import pallas as pl
from jax.experimental.pallas import tpu as pltpu
from jax.sharding import PartitionSpec as P

HEAD_DIM = 64
EPSILON = 1e-06
SCORE_SCALE = 0.125 * 1.4426950408889634
bf16, f32 = jnp.bfloat16, jnp.float32

NN = (((1,), (0,)), ((), ()))
NT = (((1,), (1,)), ((), ()))
TN = (((0,), (0,)), ((), ()))


def dot(left, right, dims=NN):
    return lax.dot_general(left, right, dims, preferred_element_type=f32)


def sds(shape, dtype):
    return jax.ShapeDtypeStruct(shape, dtype)


def whole(shape):
    return pl.BlockSpec(shape, lambda *_: (0,) * len(shape))


def kernel_call(body, grid, ids, ins, outs, scratch=(), flops=0, moved=0, vmem=56):
    in_specs = [whole(a.shape) if sp is None else sp for a, sp in ins]
    out_specs = [whole(sh) if sp is None else sp for sh, _, sp in outs]
    return pl.pallas_call(
        body,
        grid_spec=pltpu.PrefetchScalarGridSpec(
            num_scalar_prefetch=1,
            grid=grid,
            in_specs=in_specs,
            out_specs=out_specs,
            scratch_shapes=list(scratch),
        ),
        out_shape=[sds(sh, dt) for sh, dt, _ in outs],
        compiler_params=pltpu.CompilerParams(
            vmem_limit_bytes=vmem << 20, dimension_semantics=("arbitrary",) * len(grid)
        ),
        cost_estimate=pl.CostEstimate(flops=flops, bytes_accessed=moved, transcendentals=0),
    )(ids, *[a for a, _ in ins])


def swap(value, axis, step):
    size = lax.axis_size(axis)
    return lax.ppermute(value, axis, [(i, i ^ step) for i in range(size)])


def norm_scale(values):
    return lax.rsqrt(jnp.mean(values * values, axis=-1, keepdims=True) + EPSILON)


def route(ids, routes, rows, groups, capacity):
    tokens, width = rows.shape
    slots = groups * capacity

    def body(ids_ref, routes_ref, rows_ref, slot_ref, column_ref, *send_refs):
        me = ids_ref[1]
        route_row = routes_ref[...]
        named = lax.broadcasted_iota(jnp.int32, (groups, tokens), 0) == route_row
        ones = jnp.where(named, 1.0, 0.0)
        earlier = lax.broadcasted_iota(jnp.int32, (tokens, tokens), 0)
        later = lax.broadcasted_iota(jnp.int32, (tokens, tokens), 1)
        upto = jnp.where(earlier <= later, 1.0, 0.0)
        count = dot(ones, upto)
        place = jnp.sum(count * ones, axis=0, keepdims=True) - 1.0
        slot = (route_row ^ me) * capacity + place.astype(jnp.int32)
        slot_ref[...] = slot
        column_ref[...] = jnp.transpose(jnp.broadcast_to(slot.astype(f32), (128, tokens)))
        pick = lax.broadcasted_iota(jnp.int32, (slots, tokens), 0) == slot
        laid = dot(jnp.where(pick, 1.0, 0.0).astype(bf16), rows_ref[...])
        for k in range(groups):
            send_refs[k][...] = laid[k * capacity : (k + 1) * capacity].astype(bf16)

    out = kernel_call(
        body,
        (1,),
        ids,
        [(routes, None), (rows, None)],
        [((1, tokens), jnp.int32, None), ((tokens, 128), f32, None)]
        + [((capacity, width), bf16, None)] * groups,
        flops=2 * slots * tokens * width,
        moved=4 << 20,
    )
    return out[0], out[1], out[2:]


def one_hot_columns(column, slots):
    wide = jnp.concatenate([column] * (slots // 128), axis=1)
    lanes = lax.broadcasted_iota(jnp.int32, wide.shape, 1).astype(f32)
    return jnp.where(wide == lanes, 1.0, 0.0).astype(bf16)


def project(ids, rows, gain, weight):
    tokens, width = rows.shape
    part = width // lax.axis_size("seq")
    heads = width // part

    def body(ids_ref, x_ref, gain_ref, wq_ref, wk_ref, wv_ref, n_ref, q_ref, k_ref, v_ref):
        values = x_ref[...].astype(f32)
        normed = (values * norm_scale(values) * gain_ref[...]).astype(bf16)
        n_ref[...] = normed
        q_ref[...] = dot(normed, wq_ref[...]).astype(bf16)
        k_ref[...] = dot(normed, wk_ref[...]).astype(bf16)
        v_ref[...] = dot(normed, wv_ref[...]).astype(bf16)

    half = tokens // 2
    column = lambda which: pl.BlockSpec((width, part), lambda i, d: (0, d[0] + which * heads))
    row_spec = lambda n: pl.BlockSpec((half, n), lambda i, d: (i, 0))
    return kernel_call(
        body,
        (2,),
        ids,
        [(rows, row_spec(width)), (gain, None)] + [(weight, column(w)) for w in range(3)],
        [((tokens, width), bf16, row_spec(width))]
        + [((tokens, part), bf16, row_spec(part))] * 3,
        flops=6 * tokens * width * part,
        moved=5 << 20,
    )


def head_lanes(block, head):
    lanes = lax.broadcasted_iota(jnp.int32, block.shape, 1)
    inside = (lanes >= head * HEAD_DIM) & (lanes < (head + 1) * HEAD_DIM)
    return jnp.where(inside, block, jnp.zeros_like(block))


def fold_rows(values, how):
    return how(values.reshape(values.shape[0] // 8, 8, values.shape[1]), axis=0)


def attention(ids, queries, keys, values):
    blocks = len(queries)
    tokens, part = queries[0].shape
    length = tokens // 2
    heads = part // HEAD_DIM
    total = blocks * length

    def body(ids_ref, *refs):
        ins, refs = refs[: 3 * blocks], refs[3 * blocks :]
        out_refs, refs = refs[:blocks], refs[blocks:]
        ot_ref, lse_ref, q_all, k_all, vt_all, stacked, scores, result = refs
        me = ids_ref[0]
        for j in range(blocks):
            rows = pl.ds(pl.multiple_of((me ^ j) * length, length), length)
            q_all[rows, :] = ins[j][...]
            k_all[rows, :] = ins[blocks + j][...]
            vt_all[:, rows] = jnp.transpose(ins[2 * blocks + j][...].astype(f32)).astype(bf16)
        hidden = lax.broadcasted_iota(jnp.int32, (length, length), 0) > lax.broadcasted_iota(
            jnp.int32, (length, length), 1
        )
        for qa in range(blocks):
            here = slice(qa * length, (qa + 1) * length)
            q_block = q_all[here, :]
            for h in range(heads):
                stacked[h * length : (h + 1) * length, :] = head_lanes(q_block, h)
            for h in range(heads):
                lanes = slice(h * length, (h + 1) * length)
                most = None
                for kb in range(qa + 1):
                    there = slice(kb * length, (kb + 1) * length)
                    found = dot(k_all[there, :], stacked[lanes, :], NT)
                    if kb == qa:
                        found = jnp.where(hidden, -1e30, found)
                    scores[there, lanes] = found
                    top = fold_rows(found, jnp.max)
                    most = top if most is None else jnp.maximum(most, top)
                peak = jnp.max(most, axis=0, keepdims=True) * SCORE_SCALE
                summed, gathered = None, None
                for kb in range(qa + 1):
                    there = slice(kb * length, (kb + 1) * length)
                    raised = jnp.exp2(scores[there, lanes] * SCORE_SCALE - peak)
                    part_sum = fold_rows(raised, jnp.sum)
                    summed = part_sum if summed is None else summed + part_sum
                    piece = dot(
                        vt_all[h * HEAD_DIM : (h + 1) * HEAD_DIM, there], raised.astype(bf16)
                    )
                    gathered = piece if gathered is None else gathered + piece
                weight = jnp.sum(summed, axis=0, keepdims=True)
                ot_ref[0, h * HEAD_DIM : (h + 1) * HEAD_DIM, here] = gathered * (1.0 / weight)
                lse_ref[0, qa : qa + 1, lanes] = peak + jnp.log2(weight)
            result[here, :] = jnp.transpose(ot_ref[0, :, here]).astype(bf16)
        for j in range(blocks):
            rows = pl.ds(pl.multiple_of((me ^ j) * length, length), length)
            out_refs[j][...] = result[rows, :]

    spec = pl.BlockSpec((length, part), lambda i, d: (i, 0))
    out = kernel_call(
        body,
        (2,),
        ids,
        [(a, spec) for a in (*queries, *keys, *values)],
        [((tokens, part), bf16, spec)] * blocks
        + [
            ((2, part, total), f32, pl.BlockSpec((1, part, total), lambda i, d: (i, 0, 0))),
            (
                (2, blocks, heads * length),
                f32,
                pl.BlockSpec((1, blocks, heads * length), lambda i, d: (i, 0, 0)),
            ),
        ],
        [
            pltpu.VMEM((total, part), bf16),
            pltpu.VMEM((total, part), bf16),
            pltpu.VMEM((part, total), bf16),
            pltpu.VMEM((heads * length, part), bf16),
            pltpu.VMEM((total, heads * length), f32),
            pltpu.VMEM((total, part), bf16),
        ],
        flops=2 * 10 * heads * 4 * length * length * part,
        moved=8 << 20,
    )
    return out[:blocks], out[blocks], out[blocks + 1]


def attention_back(ids, queries, keys, values, grads, ot, lse):
    blocks = len(queries)
    tokens, part = queries[0].shape
    length = tokens // 2
    heads = part // HEAD_DIM
    total = blocks * length

    def body(ids_ref, *refs):
        ins, refs = refs[: 4 * blocks], refs[4 * blocks :]
        ot_ref, lse_ref, refs = refs[0], refs[1], refs[2:]
        out_refs, refs = refs[:blocks], refs[blocks:]
        q_all, k_all, v_all, g_all, kt_all, q_stack, g_stack, low, ds_low, dk, dv, dqt, dq = refs
        me = ids_ref[0]
        for j in range(blocks):
            rows = pl.ds(pl.multiple_of((me ^ j) * length, length), length)
            q_all[rows, :] = ins[j][...]
            k_all[rows, :] = ins[blocks + j][...]
            v_all[rows, :] = ins[2 * blocks + j][...]
            g_all[rows, :] = ins[3 * blocks + j][...]
            kt_all[:, rows] = jnp.transpose(ins[blocks + j][...].astype(f32)).astype(bf16)
        dk[...] = jnp.zeros_like(dk)
        dv[...] = jnp.zeros_like(dv)
        hidden = lax.broadcasted_iota(jnp.int32, (length, length), 0) > lax.broadcasted_iota(
            jnp.int32, (length, length), 1
        )
        for qa in range(blocks):
            here = slice(qa * length, (qa + 1) * length)
            q_block, g_block = q_all[here, :], g_all[here, :]
            for h in range(heads):
                lanes = slice(h * length, (h + 1) * length)
                q_stack[lanes, :] = head_lanes(q_block, h)
                g_stack[lanes, :] = head_lanes(g_block, h)
            product = jnp.transpose(g_block.astype(f32)) * ot_ref[0, :, here]
            totals = [
                jnp.sum(product[h * HEAD_DIM : (h + 1) * HEAD_DIM], axis=0, keepdims=True)
                for h in range(heads)
            ]
            for kb in range(qa + 1):
                there = slice(kb * length, (kb + 1) * length)
                for h in range(heads):
                    lanes = slice(h * length, (h + 1) * length)
                    found = dot(k_all[there, :], q_stack[lanes, :], NT)
                    if kb == qa:
                        found = jnp.where(hidden, -1e30, found)
                    probs = jnp.exp2(found * SCORE_SCALE - lse_ref[0, qa : qa + 1, lanes])
                    grad_probs = dot(v_all[there, :], g_stack[lanes, :], NT)
                    low[:, lanes] = probs.astype(bf16)
                    ds_low[:, lanes] = (probs * (grad_probs - totals[h])).astype(bf16)
                dv[there, :] += dot(low[...], g_stack[...])
                dk[there, :] += dot(ds_low[...], q_stack[...])
                for h in range(heads):
                    lanes = slice(h * length, (h + 1) * length)
                    rows = slice(h * HEAD_DIM, (h + 1) * HEAD_DIM)
                    piece = dot(kt_all[rows, there], ds_low[:, lanes])
                    if kb == 0:
                        dqt[rows, :] = piece
                    else:
                        dqt[rows, :] += piece
            dq[here, :] = (0.125 * jnp.transpose(dqt[...])).astype(bf16)
        for j in range(blocks):
            rows = pl.ds(pl.multiple_of((me ^ j) * length, length), length)
            out_refs[j][:, 0:part] = dq[rows, :]
            out_refs[j][:, part : 2 * part] = (0.125 * dk[rows, :]).astype(bf16)
            out_refs[j][:, 2 * part : 3 * part] = dv[rows, :].astype(bf16)

    spec = pl.BlockSpec((length, part), lambda i, d: (i, 0))
    return kernel_call(
        body,
        (2,),
        ids,
        [(a, spec) for a in (*queries, *keys, *values, *grads)]
        + [
            (ot, pl.BlockSpec((1, part, total), lambda i, d: (i, 0, 0))),
            (lse, pl.BlockSpec((1, blocks, heads * length), lambda i, d: (i, 0, 0))),
        ],
        [((tokens, 3 * part), bf16, pl.BlockSpec((length, 3 * part), lambda i, d: (i, 0)))]
        * blocks,
        [pltpu.VMEM((total, part), bf16)] * 4
        + [
            pltpu.VMEM((part, total), bf16),
            pltpu.VMEM((heads * length, part), bf16),
            pltpu.VMEM((heads * length, part), bf16),
            pltpu.VMEM((length, heads * length), bf16),
            pltpu.VMEM((length, heads * length), bf16),
            pltpu.VMEM((total, part), f32),
            pltpu.VMEM((total, part), f32),
            pltpu.VMEM((part, length), f32),
            pltpu.VMEM((total, part), bf16),
        ],
        flops=2 * 10 * heads * 10 * length * length * part,
        moved=10 << 20,
    )


def head_rows(weight, j):
    part = weight.shape[0] // lax.axis_size("seq")
    return (weight, pl.BlockSpec((part, weight.shape[1]), lambda i, d: (d[0] ^ j, 0)))


def attention_out(ids, rows, attended, weight, gain, slot, groups, capacity):
    tokens, width = rows.shape
    slots = groups * capacity
    blocks = len(attended)

    def body(ids_ref, x_ref, gain_ref, slot_ref, *refs):
        att, weights, refs = refs[:blocks], refs[blocks : 2 * blocks], refs[2 * blocks :]
        h_ref, send_refs = refs[0], refs[1:]
        hidden = x_ref[...].astype(f32)
        for j in range(blocks):
            hidden += dot(att[j][...], weights[j][...])
        h_ref[...] = hidden
        normed = (hidden * norm_scale(hidden) * gain_ref[...]).astype(bf16)
        pick = lax.broadcasted_iota(jnp.int32, (slots, tokens), 0) == slot_ref[...]
        laid = dot(jnp.where(pick, 1.0, 0.0).astype(bf16), normed)
        for k in range(groups):
            send_refs[k][...] = laid[k * capacity : (k + 1) * capacity].astype(bf16)

    out = kernel_call(
        body,
        (1,),
        ids,
        [(rows, None), (gain, None), (slot, None)]
        + [(a, None) for a in attended]
        + [head_rows(weight, j) for j in range(blocks)],
        [((tokens, width), f32, None)] + [((capacity, width), bf16, None)] * groups,
        flops=2 * tokens * width * width + 2 * slots * tokens * width,
        moved=9 << 20,
    )
    return out[0], out[1:]


def normal_parts(values):
    size = jnp.abs(values)
    near = 1.0 + 0.23164189 * size
    t = pl.reciprocal(near, approx=True)
    t = t * (2.0 - near * t)
    fall = jnp.exp2(values * values * -0.7213475204444817)
    tail = t * (
        0.127414796
        + t * (-0.142248368 + t * (0.7107068705 + t * (-0.7265760135 + t * 0.5307027145)))
    )
    tail = tail * fall
    below = jnp.where(values >= 0.0, 1.0 - tail, tail)
    return below, values * fall * 0.3989422804014327


def expert_grad_act(ids, grads, weight):
    groups = len(grads)
    capacity, width = grads[0].shape
    slots, hidden = groups * capacity, weight.shape[0]
    step = 512

    def body(ids_ref, *refs):
        g_refs, (w_ref, out_ref, rows) = refs[:groups], refs[groups:]

        @pl.when(pl.program_id(0) == 0)
        def _():
            for k in range(groups):
                rows[k * capacity : (k + 1) * capacity, :] = g_refs[k][...]

        out_ref[...] = dot(rows[...], w_ref[...], NT)

    return kernel_call(
        body,
        (hidden // step,),
        ids,
        [(g, None) for g in grads] + [(weight, pl.BlockSpec((step, width), lambda i, d: (i, 0)))],
        [((slots, hidden), f32, pl.BlockSpec((slots, step), lambda i, d: (0, i)))],
        [pltpu.VMEM((slots, width), bf16)],
        flops=2 * slots * hidden * width,
        moved=26 << 20,
    )[0]


def expert_main(ids, rows_in, grad_act, weight):
    groups = len(rows_in)
    capacity, width = rows_in[0].shape
    slots, hidden = groups * capacity, weight.shape[0]
    step, chunk = 512, 256

    def body(ids_ref, *refs):
        x_refs, (ga_ref, w_ref, act_ref, gp_ref), refs = (
            refs[:groups],
            refs[groups : groups + 4],
            refs[groups + 4 :],
        )
        out_refs, (rows, total) = refs[:groups], refs[groups:]
        here = pl.program_id(0)

        @pl.when(here == 0)
        def _():
            for k in range(groups):
                rows[k * capacity : (k + 1) * capacity, :] = x_refs[k][...]
            total[...] = jnp.zeros_like(total)

        for r in range(slots // chunk):
            part = slice(r * chunk, (r + 1) * chunk)
            pre = dot(rows[part, :], w_ref[...], NT)
            below, dense = normal_parts(pre)
            act_ref[part, :] = (pre * below).astype(bf16)
            grad_pre = (ga_ref[part, :] * (below + dense)).astype(bf16)
            gp_ref[part, :] = grad_pre
            total[part, :] += dot(grad_pre, w_ref[...])

        @pl.when(here == pl.num_programs(0) - 1)
        def _():
            for k in range(groups):
                out_refs[k][...] = total[k * capacity : (k + 1) * capacity, :].astype(bf16)

    wide = pl.BlockSpec((slots, step), lambda i, d: (0, i))
    out = kernel_call(
        body,
        (hidden // step,),
        ids,
        [(x, None) for x in rows_in]
        + [(grad_act, wide), (weight, pl.BlockSpec((step, width), lambda i, d: (i, 0)))],
        [((slots, hidden), bf16, wide)] * 2 + [((capacity, width), bf16, None)] * groups,
        [pltpu.VMEM((slots, width), bf16), pltpu.VMEM((slots, width), f32)],
        flops=4 * slots * hidden * width,
        moved=44 << 20,
    )
    return out[0], out[1], out[2:]


def block_result(ids, hidden, returned, column):
    tokens, width = hidden.shape
    groups, capacity = len(returned), returned[0].shape[0]

    def body(ids_ref, h_ref, c_ref, *refs):
        back, (out_ref, rows) = refs[:groups], refs[groups:]
        for k in range(groups):
            rows[k * capacity : (k + 1) * capacity, :] = back[k][...]
        pick = one_hot_columns(c_ref[...], groups * capacity)
        out_ref[...] = (h_ref[...] + dot(pick, rows[...])).astype(bf16)

    return kernel_call(
        body,
        (1,),
        ids,
        [(hidden, None), (column, None)] + [(a, None) for a in returned],
        [((tokens, width), bf16, None)],
        [pltpu.VMEM((groups * capacity, width), bf16)],
        flops=2 * groups * capacity * tokens * width,
        moved=5 << 20,
    )[0]


def norm_back(values, gain, grads):
    scale = norm_scale(values)
    scaled = grads * gain
    along = jnp.mean(values * scaled, axis=-1, keepdims=True)
    through = scale * scaled - values * (scale * scale * scale * along)
    return through, jnp.sum(grads * (values * scale), axis=0, keepdims=True)


def hidden_back(ids, hidden, cotangent, gain, returned, column, weight):
    tokens, width = hidden.shape
    groups, capacity = len(returned), returned[0].shape[0]
    blocks = lax.axis_size("seq")
    part = width // blocks

    def body(ids_ref, h_ref, c_ref, gain_ref, col_ref, *refs):
        back, weights, refs = refs[:groups], refs[groups : groups + blocks], refs[groups + blocks :]
        gh_ref, gb_ref, gain_out, refs = refs[0], refs[1], refs[2], refs[3:]
        out_refs, rows = refs[:blocks], refs[blocks]
        for k in range(groups):
            rows[k * capacity : (k + 1) * capacity, :] = back[k][...]
        pick = one_hot_columns(col_ref[...], groups * capacity)
        grads = dot(pick, rows[...])
        through, gain_grad = norm_back(h_ref[...], gain_ref[...], grads)
        grad_hidden = c_ref[...].astype(f32) + through
        gh_ref[...] = grad_hidden
        low = grad_hidden.astype(bf16)
        gb_ref[...] = low
        gain_out[...] = gain_grad
        for j in range(blocks):
            out_refs[j][...] = dot(low, weights[j][...], NT).astype(bf16)

    out = kernel_call(
        body,
        (1,),
        ids,
        [(hidden, None), (cotangent, None), (gain, None), (column, None)]
        + [(a, None) for a in returned]
        + [head_rows(weight, j) for j in range(blocks)],
        [((tokens, width), f32, None), ((tokens, width), bf16, None), ((1, width), f32, None)]
        + [((tokens, part), bf16, None)] * blocks,
        [pltpu.VMEM((groups * capacity, width), bf16)],
        flops=2 * groups * capacity * tokens * width + 2 * tokens * width * width,
        moved=11 << 20,
    )
    return out[0], out[1], out[2], out[3:]


def projection_back(ids, grads, weight):
    blocks = len(grads)
    tokens = grads[0].shape[0]
    width = weight.shape[0]
    part = grads[0].shape[1] // 3
    heads = width // part
    kinds = [f32 if j % 2 == 0 else bf16 for j in range(blocks)]

    def body(ids_ref, *refs):
        g_refs, w_refs, out_refs = refs[:blocks], refs[blocks : blocks + 3], refs[blocks + 3 :]
        for j in (1, 3, 2, 0):
            total = None
            for w in range(3):
                piece = dot(g_refs[j][:, w * part : (w + 1) * part], w_refs[w][...], NT)
                total = piece if total is None else total + piece
            out_refs[j][...] = total.astype(kinds[j])

    column = lambda which: pl.BlockSpec((width, part), lambda i, d: (0, d[0] + which * heads))
    return kernel_call(
        body,
        (1,),
        ids,
        [(g, None) for g in grads] + [(weight, column(w)) for w in range(3)],
        [((tokens, width), kind, None) for kind in kinds],
        flops=2 * blocks * tokens * width * 3 * part,
        moved=12 << 20,
    )


def projection_grad(ids, normed, grads, groups):
    blocks = len(grads)
    tokens, width = normed[0].shape
    columns = grads[0].shape[1]
    rows = width // groups

    def body(ids_ref, *refs):
        n_refs, g_refs, refs = refs[:blocks], refs[blocks : 2 * blocks], refs[2 * blocks :]
        out_refs, total = refs[:groups], refs[groups]
        me = ids_ref[1]
        for j in range(blocks):
            piece = dot(n_refs[j][...], g_refs[j][...], TN)
            if j == 0:
                total[...] = piece
            else:
                total[...] += piece
        for k in range(groups):
            here = pl.ds(pl.multiple_of((me ^ k) * rows, rows), rows)
            out_refs[k][...] = total[here, :].astype(bf16)

    return kernel_call(
        body,
        (1,),
        ids,
        [(a, None) for a in (*normed, *grads)],
        [((rows, columns), bf16, None)] * groups,
        [pltpu.VMEM((width, columns), f32)],
        flops=2 * blocks * tokens * width * columns,
        moved=10 << 20,
    )


def input_back(ids, rows, gain, grad_hidden, pieces):
    tokens, width = rows.shape

    def body(ids_ref, x_ref, gain_ref, gh_ref, a_ref, b_ref, c_ref, out_ref, gain_out):
        grads = a_ref[...] + b_ref[...].astype(f32) + c_ref[...].astype(f32)
        through, gain_grad = norm_back(x_ref[...].astype(f32), gain_ref[...], grads)
        out_ref[...] = gh_ref[...] + through
        gain_out[...] = gain_grad

    return kernel_call(
        body,
        (1,),
        ids,
        [(rows, None), (gain, None), (grad_hidden, None)] + [(a, None) for a in pieces],
        [((tokens, width), f32, None), ((1, width), f32, None)],
        flops=0,
        moved=10 << 20,
    )


def sum_over_seq(parts):
    near_1 = swap(parts[1].astype(bf16), "seq", 1)
    near_3 = swap(parts[3].astype(bf16), "seq", 1)
    far = (parts[2] + near_3.astype(f32)).astype(bf16)
    return parts[0], near_1, swap(far, "seq", 2)


def sum_over_expert(pieces):
    groups = len(pieces)
    total = pieces[0].astype(f32)
    for k in range(1, groups):
        total += swap(pieces[k], "expert", k).astype(f32)
    return total


def sum_everywhere(value):
    for axis in ("seq", "expert"):
        step = 1
        while step < lax.axis_size(axis):
            value = value + swap(value, axis, step)
            step *= 2
    return value


def shards(
    inputs,
    query_key_value_weight,
    output_weight,
    gain_attn,
    gain_ffn,
    w_up,
    w_down,
    expert_of,
    cotangent,
):
    groups = lax.axis_size("expert")
    blocks = lax.axis_size("seq")
    seq_count, local_len, width = inputs.shape
    tokens = seq_count * local_len
    capacity = max(2, 2 * tokens // groups)
    ids = jnp.stack([lax.axis_index("seq"), lax.axis_index("expert")]).astype(jnp.int32)
    gain_a, gain_f = gain_attn.reshape(1, width), gain_ffn.reshape(1, width)
    rows = inputs.reshape(tokens, width)
    cot = cotangent.reshape(tokens, width)

    rows_2 = swap(rows, "seq", 2)
    rows_1 = swap(rows, "seq", 1)
    rows_3 = swap(rows_2, "seq", 1)
    all_rows = [rows, rows_1, rows_2, rows_3]

    slot, column, send = route(ids, expert_of.reshape(1, tokens), cot, groups, capacity)
    grads_in = [send[0]] + [swap(send[k], "expert", k) for k in range(1, groups)]

    def all_units(weight, after):
        weight = weight[0]
        weight, _ = lax.optimization_barrier((weight, after))
        far = swap(weight, "seq", 2)
        return jnp.concatenate([weight, swap(weight, "seq", 1), far, swap(far, "seq", 1)], axis=0)

    down_all = all_units(w_down, rows_2)
    up_all = all_units(w_up, down_all)
    grad_act = expert_grad_act(ids, grads_in, down_all)

    projected = [project(ids, r, gain_a, query_key_value_weight) for r in all_rows]
    normed, queries, keys, values = (list(p) for p in zip(*projected))
    out, ot, lse = attention(ids, queries, keys, values)
    attended = [out[0]] + [swap(out[j], "seq", j) for j in range(1, blocks)]
    hidden, send = attention_out(
        ids, rows, attended, output_weight, gain_f, slot, groups, capacity
    )
    rows_in = [send[0]] + [swap(send[k], "expert", k) for k in range(1, groups)]

    activated, grad_pre, back = expert_main(ids, rows_in, grad_act, up_all)
    returned_grad = [back[0]] + [swap(back[k], "expert", k) for k in range(1, groups)]
    expert_out = dot(activated, down_all).astype(bf16)
    outs = [expert_out[k * capacity : (k + 1) * capacity] for k in range(groups)]
    returned = [outs[0]] + [swap(outs[k], "expert", k) for k in range(1, groups)]
    units = grad_pre.shape[1] // blocks
    rows_cat, grads_cat = jnp.concatenate(rows_in, axis=0), jnp.concatenate(grads_in, axis=0)

    def unit_grads(left, right):
        cuts = [left[:, j * units : (j + 1) * units] for j in range(blocks)]
        own, near, far = sum_over_seq([dot(c, right, TN) for c in cuts])
        return (own + near.astype(f32) + far.astype(f32))[None]

    up_grad = unit_grads(grad_pre, rows_cat)
    down_grad = unit_grads(activated, grads_cat)

    block_out = block_result(ids, hidden, returned, column)
    grad_hidden, low, ffn_gain_part, grad_att = hidden_back(
        ids, hidden, cot, gain_f, returned_grad, column, output_weight
    )
    grad_att = [grad_att[0]] + [swap(grad_att[j], "seq", j) for j in range(1, blocks)]
    own, near, far = sum_over_seq([dot(a, low, TN) for a in attended])
    out_part = own + near.astype(f32) + far.astype(f32)
    height = out_part.shape[0] // groups
    me = lax.axis_index("expert")
    out_piece = sum_over_expert(
        [
            lax.dynamic_slice_in_dim(out_part, (me ^ k) * height, height, 0).astype(bf16)
            for k in range(groups)
        ]
    ).astype(bf16)

    grad_proj = attention_back(ids, queries, keys, values, grad_att, ot, lse)
    grad_normed = sum_over_seq(projection_back(ids, grad_proj, query_key_value_weight))
    input_grad, attn_gain_part = input_back(ids, rows, gain_a, grad_hidden, grad_normed)
    qkv_piece = sum_over_expert(projection_grad(ids, normed, grad_proj, groups)).astype(bf16)

    part = width // blocks
    high = width // groups
    gathered = lax.all_gather(qkv_piece, ("expert", "seq"), axis=0, tiled=False)
    gathered = gathered.reshape(groups, blocks, high, 3, part).transpose(0, 2, 3, 1, 4)
    qkv_grad = gathered.reshape(width, 3 * width).astype(f32)
    gathered = lax.all_gather(out_piece, ("expert", "seq"), axis=0, tiled=False)
    gathered = gathered.reshape(groups, blocks, height, width).transpose(1, 0, 2, 3)
    out_grad = gathered.reshape(width, width).astype(f32)
    gains = sum_everywhere(jnp.concatenate([attn_gain_part, ffn_gain_part], axis=0))

    return (
        block_out.reshape(inputs.shape),
        input_grad.reshape(inputs.shape),
        qkv_grad,
        out_grad,
        gains[0],
        gains[1],
        up_grad,
        down_grad,
    )


def solution(mesh):
    tokens = P("expert", "seq", None)
    units = P("expert", "seq", None)
    in_specs = (tokens, P(), P(), P(), P(), units, units, P("expert", "seq"), tokens)
    out_specs = (tokens, tokens, P(), P(), P(), P(), units, units)
    return jax.shard_map(shards, mesh=mesh, in_specs=in_specs, out_specs=out_specs, check_vma=False)
```

time: 1430 us -> 780 us (0.55)
  waiting for transfers between devices: 694 us -> 294 us
  matrix products: 367 us -> 60.5 us
  Pallas kernels: 0 us -> 157 us
  starting transfers between devices: 20.6 us -> 135 us
  other arithmetic: 141 us -> 40.5 us
  blocking collectives: 92.9 us -> 0 us
  local copies, waits for them, and re-layouts: 98.3 us -> 72.6 us
    reduce_scatter x4 -> x0, waiting for transfers between devices: 315 us -> none  [the longest x1 129 us: expert_backward(): lax.psum_scatter(up_full, 'seq', scatter_dimension=0, tiled=True)]
    dot_general x23 -> x13, matrix products: 367 us -> 60.5 us  [dot(): return lax.dot_general(left, right, dims, preferred_element_type=f32)]
    ppermute x0 -> x74, waiting for transfers between devices: none -> 294 us  [swap(): return lax.ppermute(value, axis, [(i, i ^ step) for i in range(size)])]
    psum x1 -> x0, waiting for transfers between devices: 182 us -> none  [backward(): lax.psum((qkv_grad, out_grad, attn_gain_grad, ffn_gain_grad), ('expert',...]
    pallas_call x0 -> x15, Pallas kernels: none -> 157 us  [kernel_call(): pl.pallas_call(body, grid_spec=pltpu.PrefetchScalarGridSpec(num_scalar_pr...]
    all_to_all x4 -> x0, waiting for transfers between devices: 141 us -> none  [the longest x3 93.4 us: to_experts(): lax.all_to_all(slots_in, 'expert', split_axis=0, concat_axis=0, tiled=True)]
    ppermute x0 -> x74, starting transfers between devices: none -> 135 us  [swap(): return lax.ppermute(value, axis, [(i, i ^ step) for i in range(size)])]
    sub x3 -> x0, other arithmetic: 78.1 us -> none  [the longest x2 78 us: probabilities(): raised = jnp.exp(scores - row_max)]
  transfers between devices with their start and end apart: 15 -> 76, of which waited for: 10 -> 30; matrix products, arithmetic and copies ran while one was open for 28% -> 14% of each run, Pallas kernels for 0% -> 14%
where the time goes in v1:
time: 780 us; the launch traced here: 775 us
  waiting for transfers between devices  294 us (38%)
  Pallas kernels  157 us (20%)
  starting transfers between devices  135 us (17%)
  local copies, waits for them, and re-layouts  72.6 us (9%)
  matrix products  60.5 us (8%)
  other arithmetic  40.5 us (5%)
  between operations  15.2 us (2%)
    ppermute x74, waiting for transfers between devices, swap(): return lax.ppermute(value, axis, [(i, i ^ step) for i in range(size)])  294 us
    pallas_call x15, Pallas kernels, kernel_call(): pl.pallas_call(body, grid_spec=pltpu.PrefetchScalarGridSpec(num_scalar_pr...  157 us
    ppermute x74, starting transfers between devices, swap(): return lax.ppermute(value, axis, [(i, i ^ step) for i in range(size)])  135 us
    dot_general x13, matrix products, dot(): return lax.dot_general(left, right, dims, preferred_element_type=f32)  60.5 us
    unnamed x168, local copies, waits for them, and re-layouts  42.4 us
    convert_element_type x2, local copies, waits for them, and re-layouts, shards(): qkv_grad = gathered.reshape(width, 3 * width).astype(f32)  25 us
    concatenate x1, other arithmetic, all_units(): jnp.concatenate([weight, swap(weight, 'seq', 1), far, swap(far, 'seq', 1)...  22.5 us
  transfers between devices with their start and end apart: 76, of which 30 were waited for; matrix products, arithmetic and copies ran while one was open for 14% of the time, Pallas kernels for 14%

profile of v1, /device:TPU:0, one launch (start us, length us, event | category | flops | bytes accessed | tf_op | source)
XLA Modules:
  0.0 774.7 jit_solution(3441228345658706091)
XLA Ops:
  7.2 3.0 collective-permute-start.1
  10.2 23.5 %collective-permute-done.1.x_ref = bf16[512,1024]{1,0:T(8,128)(2,1)} collective-permute-done((bf16[512,1024]{1,0:T(8,128)(2,1)}, bf16[512,1024]{1,0:T(8,128)(2,1)}, u32[]{:S(2)}, u32[]{:S(2)}) %collective-permute-start.1) | collective-permute-done | bytes 1048608 | tf_op jit(solution)/shard_map/ppermute | solution.py:52
  35.4 45.3 %collective-permute-done.21 = bf16[1024,1024]{1,0:T(8,128)(2,1)S(1)} collective-permute-done((bf16[1024,1024]{1,0:T(8,128)(2,1)}, bf16[1024,1024]{1,0:T(8,128)(2,1)S(1)}, u32[]{:S(2)}, u32[]{:S(2)}) %collective-permute-start.21) | collective-permute-done | bytes 2097184 | tf_op jit(solution)/shard_map/ppermute | solution.py:52
  89.8 4.5 shard_map.152
  95.9 37.0 %collective-permute-done.24 = bf16[1024,1024]{1,0:T(8,128)(2,1)} collective-permute-done((bf16[1024,1024]{1,0:T(8,128)(2,1)S(1)}, bf16[1024,1024]{1,0:T(8,128)(2,1)}, u32[]{:S(2)}, u32[]{:S(2)}) %collective-permute-start.24) | collective-permute-done | bytes 2097184 | tf_op jit(solution)/shard_map/ppermute | solution.py:52
  132.9 4.5 shard_map.153
  137.4 4.5 shard_map.155
  143.6 4.3 shard_map.154
  149.4 4.4 shard_map.156
  153.8 2.7 collective-permute-start.16
  156.5 15.4 %shard_map.157 = (bf16[512,256]{1,0:T(8,128)(2,1)}, bf16[512,256]{1,0:T(8,128)(2,1)}, bf16[512,256]{1,0:T(8,128)(2,1)}, bf16[512,256]{1,0:T(8,128)(2,1)}, f32[2,...) custom-call(s32[2]{0:T(128)} %pad_add_fusion.ids_ref, bf16[512,256]{1,0:T(8,128)(2,1)} %get-tuple-element.87.refs_0_, ...), custom_call_target="tpu_custom_call" | custom-call | flops 5368709120 | bytes 8388608 | tf_op jit(solution)/shard_map/pallas_call | solution.py:33
  174.2 7.2 collective-permute-done.4.refs_2_
  182.8 3.3 collective-permute-done.5.refs_3_
  187.4 7.2 shard_map.158
  194.6 7.3 collective-permute-done.17.refs_5_
  202.4 4.8 collective-permute-start.7
  207.2 6.1 collective-permute-start.8
  213.3 16.7 %shard_map.159.refs_8_ = f32[1024,4096]{1,0:T(8,128)} custom-call(s32[2]{0:T(128)} %pad_add_fusion.ids_ref, bf16[128,1024]{1,0:T(8,128)(2,1)} %get-tuple-element.113.refs_0_, bf16[128,1024]{1,0:T(8,128)(2,1)} %copy-done.29, bf16[128,1024]{1,0:T(8,128)(2,1)} %copy-done.31, bf16[128,1024]{1,0:T(8,128)(2,1)} %copy-done.33, bf16[128,1024]{1,0:T(8,128)(2,1)} %copy-done.35, ...), custom_call_target="tpu_custom_call" | custom-call | flops 8589934592 | bytes 27262976 | tf_op jit(solution)/shard_map/pallas_call | solution.py:33
  230.0 3.8 collective-permute-start.10
  237.7 22.5 %pad_maximum_fusion.refs_9_ = bf16[4096,1024]{1,0:T(8,128)(2,1)} fusion(bf16[1024,1024]{1,0:T(8,128)(2,1)S(1)} %collective-permute-done.25, bf16[1024,1024]{1,0:T(8,128)(2,1)} %collective-permute-done.24, bf16[1024,1024]{1,0:T(8,128)(2,1)S(1)} %collective-permute-done.23, bf16[1024,1024]{1,0:T(8,128)(2,1)S(1)} %bitcast.58), kind=kLoop, calls=%fused_computation | loop fusion | flops 33554432 | bytes 16777216 | tf_op jit(solution)/shard_map/concatenate | solution.py:654
  260.9 5.9 collective-permute-done.10.refs_5_
  267.7 41.4 %shard_map.160 = (bf16[1024,4096]{1,0:T(8,128)(2,1)}, bf16[1024,4096]{1,0:T(8,128)(2,1)}, bf16[128,1024]{1,0:T(8,128)(2,1)}, bf16[128,1024]{1,0:T(8,128)(2,1)}, ...) custom-call(s32[2]{0:T(128)} %pad_add_fusion.ids_ref, ...), custom_call_target="tpu_custom_call" | custom-call | flops 17179869184 | bytes 46137344 | tf_op jit(solution)/shard_map/pallas_call | solution.py:33
  310.3 11.5 %collective-permute-start.34 = (bf16[128,1024]{1,0:T(8,128)(2,1)}, bf16[128,1024]{1,0:T(8,128)(2,1)S(1)}, u32[]{:S(2)}, u32[]{:S(2)}) collective-permute-start(bf16[128,1024]{1,0:T(8,128)(2,1)} %get-tuple-element.126), channel_id=1, source_target_pairs={{0,8},{4,12},{8,0},{12,4},{16,24},{20,28},{24,16},{28,20},{1,9},{5... | collective-permute-start | bytes 786440 | tf_op jit(solution)/shard_map/ppermute | solution.py:52
  322.1 2.6 collective-permute-start.36
  327.4 11.7 %collective-permute-done.34.refs_2_ = bf16[128,1024]{1,0:T(8,128)(2,1)S(1)} collective-permute-done((bf16[128,1024]{1,0:T(8,128)(2,1)}, bf16[128,1024]{1,0:T(8,128)(2,1)S(1)}, u32[]{:S(2)}, u32[]{:S(2)}) %collective-permute-start.34) | collective-permute-done | bytes 262176 | tf_op jit(solution)/shard_map/ppermute | solution.py:52
  344.0 17.1 %collective-permute-done.37.refs_5_ = bf16[128,1024]{1,0:T(8,128)(2,1)S(1)} collective-permute-done((bf16[128,1024]{1,0:T(8,128)(2,1)}, bf16[128,1024]{1,0:T(8,128)(2,1)S(1)}, u32[]{:S(2)}, u32[]{:S(2)}) %collective-permute-start.37) | collective-permute-done | bytes 262176 | tf_op jit(solution)/shard_map/ppermute | solution.py:52
  362.1 7.8 %shard_map.162 = (f32[512,1024]{1,0:T(8,128)}, bf16[512,1024]{1,0:T(8,128)(2,1)}, f32[1,1024]{1,0:T(1,128)}, bf16[512,256]{1,0:T(8,128)(2,1)}, bf16[512,256]{1,0...) custom-call(s32[2]{0:T(128)} %pad_add_fusion.ids_ref, f32[512,1024]{1,0:T(8,128)} %get-tuple-element.103.h_ref, ...), custom_call_target="tpu_custom_call" | custom-call | flops 2147483648 | bytes 11534336 | tf_op jit(solution)/shard_map/pallas_call | solution.py:33
  376.1 12.4 %collective-permute-done.55 = bf16[256,1024]{1,0:T(8,128)(2,1)S(1)} collective-permute-done((bf16[256,1024]{1,0:T(8,128)(2,1)S(1)}, bf16[256,1024]{1,0:T(8,128)(2,1)S(1)}, u32[]{:S(2)}, u32[]{:S(2)}) %collective-permute-start.55) | collective-permute-done | bytes 524320 | tf_op jit(solution)/shard_map/ppermute | solution.py:52
  393.2 9.2 %collective-permute-start.60 = (bf16[32,1024]{1,0:T(8,128)(2,1)S(1)}, bf16[32,1024]{1,0:T(8,128)(2,1)S(1)}, u32[]{:S(2)}, u32[]{:S(2)}) collective-permute-start(bf16[32,1024]{1,0:T(8,128)(2,1)S(1)} %get-tuple-element.183), channel_id=1, source_target_pairs={{0,20},{4,16},{8,28},{12,24},{16,4},{20,0},{24,12},{28,8},{1,21},{... | collective-permute-start | bytes 196616 | tf_op jit(solution)/shard_map/ppermute | solution.py:52
  402.4 2.9 collective-permute-start.58
  413.1 7.3 collective-permute-done.41.refs_14_
  420.4 5.2 collective-permute-done.42.refs_15_
  426.3 18.7 %shard_map.163 = (bf16[512,768]{1,0:T(8,128)(2,1)}, bf16[512,768]{1,0:T(8,128)(2,1)}, bf16[512,768]{1,0:T(8,128)(2,1)}, bf16[512,768]{1,0:T(8,128)(2,1)}) custom-call(s32[2]{0:T(128)} %pad_add_fusion.ids_ref, bf16[512,256]{1,0:T(8,128)(2,1)} %get-tuple-element.87.refs_0_, bf16[512,256]{1,0:T(8,128)(2,1)} %get-tuple-element.88.refs_1_, ...), custom_call_target="tpu_custom_call" | custom-call | flops 13421772800 | bytes 10485760 | tf_op jit(solution)/shard_map/pallas_call | solution.py:33
  444.9 8.4 %shard_map.166 = (bf16[128,768]{1,0:T(8,128)(2,1)}, bf16[128,768]{1,0:T(8,128)(2,1)}, bf16[128,768]{1,0:T(8,128)(2,1)}, bf16[128,768]{1,0:T(8,128)(2,1)}, bf16[1...) custom-call(s32[2]{0:T(128)} %pad_add_fusion.ids_ref, ...), custom_call_target="tpu_custom_call" | custom-call | flops 3221225472 | bytes 10485760 | tf_op jit(solution)/shard_map/pallas_call | solution.py:33
  458.3 2.8 collective-permute-start.49
  461.4 5.2 collective-permute-done.52
  466.6 19.5 %collective-permute-start.47 = (bf16[128,768]{1,0:T(8,128)(2,1)}, bf16[128,768]{1,0:T(8,128)(2,1)S(1)}, u32[]{:S(2)}, u32[]{:S(2)}) collective-permute-start(bf16[128,768]{1,0:T(8,128)(2,1)} %get-tuple-element.154), channel_id=1, source_target_pairs={{0,8},{4,12},{8,0},{12,4},{16,24},{20,28},{24,16},{28,20},{1,9},{5... | collective-permute-start | bytes 589832 | tf_op jit(solution)/shard_map/ppermute | solution.py:52
  487.8 5.5 collective-permute-done.50
  493.2 4.4 collective-permute-done.49
  505.1 7.8 %shard_map.164 = (f32[512,1024]{1,0:T(8,128)}, bf16[512,1024]{1,0:T(8,128)(2,1)}, f32[512,1024]{1,0:T(8,128)}, bf16[512,1024]{1,0:T(8,128)(2,1)}) custom-call(s32[2]{0:T(128)} %pad_add_fusion.ids_ref, bf16[512,768]{1,0:T(8,128)(2,1)} %get-tuple-element.139.refs_0_.refs_4_, bf16[512,768]{1,0:T(8,128)(2,1)} %get-tuple-element.140.refs_1_.refs_5_, ...), custom_call_target="tpu_custom_call" | custom-call | flops 3221225472 | bytes 12582912 | tf_op jit(solution)/shard_map/pallas_call | solution.py:33
  512.9 13.9 %convolution_convert_fusion = bf16[1024,1024]{1,0:T(8,128)(2,1)S(1)} fusion(bf16[1024,4096]{1,0:T(8,128)(2,1)} %get-tuple-element.123, bf16[4096,1024]{1,0:T(8,128)(2,1)} %copy-done.13), kind=kOutput, calls=%fused_computation.23 | convolution fusion | flops 8590983168 | bytes 18874368 | tf_op jit(solution)/shard_map/dot_general | solution.py:19
  526.8 5.5 fusion.19
  534.8 5.3 fusion.25
  540.3 5.4 fusion.16
  545.7 24.2 %collective-permute-done.45.c_ref = bf16[512,1024]{1,0:T(8,128)(2,1)S(1)} collective-permute-done((bf16[512,1024]{1,0:T(8,128)(2,1)S(1)}, bf16[512,1024]{1,0:T(8,128)(2,1)S(1)}, u32[]{:S(2)}, u32[]{:S(2)}) %collective-permute-start.45) | collective-permute-done | bytes 1048608 | tf_op jit(solution)/shard_map/ppermute | solution.py:52
  570.9 6.3 shard_map.165
  577.9 5.3 fusion.22
  590.6 6.9 add_convert_fusion.1
  599.9 3.2 collective-permute-done.27.refs_2_
  604.0 3.6 collective-permute-done.28.refs_3_
  609.8 5.4 add_convert_fusion
  615.2 9.5 %collective-permute-done.30.refs_5_ = bf16[128,1024]{1,0:T(8,128)(2,1)S(1)} collective-permute-done((bf16[128,1024]{1,0:T(8,128)(2,1)S(1)}, bf16[128,1024]{1,0:T(8,128)(2,1)S(1)}, u32[]{:S(2)}, u32[]{:S(2)}) %collective-permute-start.30) | collective-permute-done | bytes 262176 | tf_op jit(solution)/shard_map/ppermute | solution.py:52
  625.1 3.8 collective-permute-start.66
  628.9 6.0 fusion.14
  639.7 5.4 collective-permute-done.32.refs_7_
  645.1 5.1 collective-permute-start.67
  650.1 5.1 shard_map.161
  656.4 6.0 add_bitcast_fusion.1
  662.5 38.5 %collective-permute-done.73 = bf16[1024,1024]{1,0:T(8,128)(2,1)} collective-permute-done((bf16[1024,1024]{1,0:T(8,128)(2,1)}, bf16[1024,1024]{1,0:T(8,128)(2,1)}, u32[]{:S(2)}, u32[]{:S(2)}) %collective-permute-start.73) | collective-permute-done | bytes 2097184 | tf_op jit(solution)/shard_map/ppermute | solution.py:52
  700.9 5.6 add_bitcast_fusion
  710.9 9.4 %copy.21 = f32[4096,768]{0,1:T(8,128)} copy(bf16[4096,768]{1,0:T(8,128)(2,1)} %all-gather.5.cloned.1.call-done) | data formatting | bytes 18874368 | tf_op jit(solution)/shard_map/convert_element_type | solution.py:710
  720.3 15.6 %reshape.58 = f32[8,4,128,3,256]{2,1,0,4,3:T(4,128)} reshape(f32[4096,768]{0,1:T(8,128)} %copy.21) | data formatting | bytes 25165824 | tf_op jit(solution)/shard_map/convert_element_type | solution.py:710
  735.9 16.1 %copy.25 = f32[8,128,3,4,256]{4,3,2,1,0:T(4,128)} copy(f32[8,128,3,4,256]{1,3,0,4,2:T(4,128)} %bitcast.45) | data formatting | bytes 25165824
  752.0 15.6 %reshape.66 = f32[1024,3072]{1,0:T(8,128)} reshape(f32[8,128,3,4,256]{4,3,2,1,0:T(4,128)} %copy.25) | data formatting | bytes 25165824
  (310 shorter events, 97.6 us)
Async XLA Ops:
  7.2 699.3 %all-gather.7.cloned.1.call-start = ((), (), s32[]{:S(2)}) async-start(), calls=%async_computation.1 | async-start | bytes 2162688 | tf_op jit(solution)/shard_map/all_gather | solution.py:711
  7.2 26.5 %collective-permute-start.1 = (bf16[512,1024]{1,0:T(8,128)(2,1)}, bf16[512,1024]{1,0:T(8,128)(2,1)}, u32[]{:S(2)}, u32[]{:S(2)}) collective-permute-start(bf16[512,1024]{1,0:T(8,128)(2,1)} %bitcast.46), channel_id=1, source_target_pairs={{0,2},{1,3},{2,0},{3,1},{4,6},{5,7},{6,4},{7,5},{8,10},{9,11},{10,... | collective-permute-start | bytes 3145736 | tf_op jit(solution)/shard_map/ppermute | solution.py:52
  33.7 47.0 %collective-permute-start.21 = (bf16[1024,1024]{1,0:T(8,128)(2,1)}, bf16[1024,1024]{1,0:T(8,128)(2,1)S(1)}, u32[]{:S(2)}, u32[]{:S(2)}) collective-permute-start(bf16[1024,1024]{1,0:T(8,128)(2,1)} %bitcast.53), channel_id=1, source_target_pairs={{0,2},{1,3},{2,0},{3,1},{4,6},{5,7},{6,4},{7,5},{8,10},{9,11},{10,... | collective-permute-start | bytes 6291464 | tf_op jit(solution)/shard_map/ppermute | solution.py:52
  35.4 47.1 %collective-permute-start.20 = (bf16[1024,1024]{1,0:T(8,128)(2,1)}, bf16[1024,1024]{1,0:T(8,128)(2,1)S(1)}, u32[]{:S(2)}, u32[]{:S(2)}) collective-permute-start(bf16[1024,1024]{1,0:T(8,128)(2,1)} %bitcast.54), channel_id=1, source_target_pairs={{0,1},{1,0},{2,3},{3,2},{4,5},{5,4},{6,7},{7,6},{8,9},{9,8},{10,11... | collective-permute-start | bytes 6291464 | tf_op jit(solution)/shard_map/ppermute | solution.py:52
  85.1 47.8 %collective-permute-start.24 = (bf16[1024,1024]{1,0:T(8,128)(2,1)S(1)}, bf16[1024,1024]{1,0:T(8,128)(2,1)}, u32[]{:S(2)}, u32[]{:S(2)}) collective-permute-start(bf16[1024,1024]{1,0:T(8,128)(2,1)S(1)} %bitcast.56), channel_id=1, source_target_pairs={{0,2},{1,3},{2,0},{3,1},{4,6},{5,7},{6,4},{7,5},{8,10},{9,11},{10,... | collective-permute-start | bytes 6291464 | tf_op jit(solution)/shard_map/ppermute | solution.py:52
  86.6 55.4 %collective-permute-start = (bf16[512,1024]{1,0:T(8,128)(2,1)S(1)}, bf16[512,1024]{1,0:T(8,128)(2,1)}, u32[]{:S(2)}, u32[]{:S(2)}) collective-permute-start(bf16[512,1024]{1,0:T(8,128)(2,1)S(1)} %bitcast.50), channel_id=1, source_target_pairs={{0,1},{1,0},{2,3},{3,2},{4,5},{5,4},{6,7},{7,6},{8,9},{9,8},{10,11... | collective-permute-start | bytes 3145736 | tf_op jit(solution)/shard_map/ppermute | solution.py:52
  88.5 59.4 %collective-permute-start.2 = (bf16[512,1024]{1,0:T(8,128)(2,1)}, bf16[512,1024]{1,0:T(8,128)(2,1)}, u32[]{:S(2)}, u32[]{:S(2)}) collective-permute-start(bf16[512,1024]{1,0:T(8,128)(2,1)} %collective-permute-done.1.x_ref), channel_id=1, source_target_pairs={{0,1},{1,0},{2,3},{3,2},{4,5},{5,4},{6,7},{7,6},{8,9},{9,8},{10,11... | collective-permute-start | bytes 3145736 | tf_op jit(solution)/shard_map/ppermute | solution.py:52
  94.3 59.4 %collective-permute-start.13 = (bf16[128,1024]{1,0:T(8,128)(2,1)}, bf16[128,1024]{1,0:T(8,128)(2,1)S(1)}, u32[]{:S(2)}, u32[]{:S(2)}) collective-permute-start(bf16[128,1024]{1,0:T(8,128)(2,1)} %get-tuple-element.114), channel_id=1, source_target_pairs={{0,4},{4,0},{8,12},{12,8},{16,20},{20,16},{24,28},{28,24},{1,5},{5... | collective-permute-start | bytes 786440 | tf_op jit(solution)/shard_map/ppermute | solution.py:52
  95.9 138.0 %collective-permute-start.23 = (bf16[1024,1024]{1,0:T(8,128)(2,1)S(1)}, bf16[1024,1024]{1,0:T(8,128)(2,1)S(1)}, u32[]{:S(2)}, u32[]{:S(2)}) collective-permute-start(bf16[1024,1024]{1,0:T(8,128)(2,1)S(1)} %bitcast.57), channel_id=1, source_target_pairs={{0,1},{1,0},{2,3},{3,2},{4,5},{5,4},{6,7},{7,6},{8,9},{9,8},{10,11... | collective-permute-start | bytes 6291464 | tf_op jit(solution)/shard_map/ppermute | solution.py:52
  132.9 102.2 %collective-permute-start.25 = (bf16[1024,1024]{1,0:T(8,128)(2,1)}, bf16[1024,1024]{1,0:T(8,128)(2,1)S(1)}, u32[]{:S(2)}, u32[]{:S(2)}) collective-permute-start(bf16[1024,1024]{1,0:T(8,128)(2,1)} %collective-permute-done.24), channel_id=1, source_target_pairs={{0,1},{1,0},{2,3},{3,2},{4,5},{5,4},{6,7},{7,6},{8,9},{9,8},{10,11... | collective-permute-start | bytes 6291464 | tf_op jit(solution)/shard_map/ppermute | solution.py:52
  142.0 29.9 %collective-permute-start.14 = (bf16[128,1024]{1,0:T(8,128)(2,1)S(1)}, bf16[128,1024]{1,0:T(8,128)(2,1)S(1)}, u32[]{:S(2)}, u32[]{:S(2)}) collective-permute-start(bf16[128,1024]{1,0:T(8,128)(2,1)S(1)} %copy-done.68), channel_id=1, source_target_pairs={{0,8},{4,12},{8,0},{12,4},{16,24},{20,28},{24,16},{28,20},{1,9},{5... | collective-permute-start | bytes 786440 | tf_op jit(solution)/shard_map/ppermute | solution.py:52
  147.9 24.1 %collective-permute-start.15 = (bf16[128,1024]{1,0:T(8,128)(2,1)S(1)}, bf16[128,1024]{1,0:T(8,128)(2,1)S(1)}, u32[]{:S(2)}, u32[]{:S(2)}) collective-permute-start(bf16[128,1024]{1,0:T(8,128)(2,1)S(1)} %copy-done.67), channel_id=1, source_target_pairs={{0,12},{4,8},{8,4},{12,0},{16,28},{20,24},{24,20},{28,16},{1,13},{... | collective-permute-start | bytes 786440 | tf_op jit(solution)/shard_map/ppermute | solution.py:52
  153.8 19.8 %collective-permute-start.16 = (bf16[128,1024]{1,0:T(8,128)(2,1)S(1)}, bf16[128,1024]{1,0:T(8,128)(2,1)S(1)}, u32[]{:S(2)}, u32[]{:S(2)}) collective-permute-start(bf16[128,1024]{1,0:T(8,128)(2,1)S(1)} %copy-done.66), channel_id=1, source_target_pairs={{0,16},{4,20},{8,24},{12,28},{16,0},{20,4},{24,8},{28,12},{1,17},{... | collective-permute-start | bytes 786440 | tf_op jit(solution)/shard_map/ppermute | solution.py:52
  172.0 9.4 %collective-permute-start.4 = (bf16[512,256]{1,0:T(8,128)(2,1)}, bf16[512,256]{1,0:T(8,128)(2,1)S(1)}, u32[]{:S(2)}, u32[]{:S(2)}) collective-permute-start(bf16[512,256]{1,0:T(8,128)(2,1)} %get-tuple-element.101), channel_id=1, source_target_pairs={{0,2},{1,3},{2,0},{3,1},{4,6},{5,7},{6,4},{7,5},{8,10},{9,11},{10,... | collective-permute-start | bytes 786440 | tf_op jit(solution)/shard_map/ppermute | solution.py:52
  173.6 12.5 %collective-permute-start.5 = (bf16[512,256]{1,0:T(8,128)(2,1)}, bf16[512,256]{1,0:T(8,128)(2,1)S(1)}, u32[]{:S(2)}, u32[]{:S(2)}) collective-permute-start(bf16[512,256]{1,0:T(8,128)(2,1)} %get-tuple-element.102), channel_id=1, source_target_pairs={{0,3},{1,2},{2,1},{3,0},{4,7},{5,6},{6,5},{7,4},{8,11},{9,10},{10,... | collective-permute-start | bytes 786440 | tf_op jit(solution)/shard_map/ppermute | solution.py:52
  173.9 28.0 %collective-permute-start.17 = (bf16[128,1024]{1,0:T(8,128)(2,1)}, bf16[128,1024]{1,0:T(8,128)(2,1)S(1)}, u32[]{:S(2)}, u32[]{:S(2)}) collective-permute-start(bf16[128,1024]{1,0:T(8,128)(2,1)} %get-tuple-element.118), channel_id=1, source_target_pairs={{0,20},{4,16},{8,28},{12,24},{16,4},{20,0},{24,12},{28,8},{1,21},{... | collective-permute-start | bytes 786440 | tf_op jit(solution)/shard_map/ppermute | solution.py:52
  181.4 21.0 %collective-permute-start.18 = (bf16[128,1024]{1,0:T(8,128)(2,1)}, bf16[128,1024]{1,0:T(8,128)(2,1)}, u32[]{:S(2)}, u32[]{:S(2)}) collective-permute-start(bf16[128,1024]{1,0:T(8,128)(2,1)} %get-tuple-element.119), channel_id=1, source_target_pairs={{0,24},{4,28},{8,16},{12,20},{16,8},{20,12},{24,0},{28,4},{1,25},{... | collective-permute-start | bytes 786440 | tf_op jit(solution)/shard_map/ppermute | solution.py:52
  186.1 21.1 %collective-permute-start.19 = (bf16[128,1024]{1,0:T(8,128)(2,1)}, bf16[128,1024]{1,0:T(8,128)(2,1)}, u32[]{:S(2)}, u32[]{:S(2)}) collective-permute-start(bf16[128,1024]{1,0:T(8,128)(2,1)} %get-tuple-element.120), channel_id=1, source_target_pairs={{0,28},{4,24},{8,20},{12,16},{16,12},{20,8},{24,4},{28,0},{1,29},{... | collective-permute-start | bytes 786440 | tf_op jit(solution)/shard_map/ppermute | solution.py:52
  201.9 28.1 %collective-permute-start.6 = (bf16[128,1024]{1,0:T(8,128)(2,1)}, bf16[128,1024]{1,0:T(8,128)(2,1)S(1)}, u32[]{:S(2)}, u32[]{:S(2)}) collective-permute-start(bf16[128,1024]{1,0:T(8,128)(2,1)} %get-tuple-element.106), channel_id=1, source_target_pairs={{0,4},{4,0},{8,12},{12,8},{16,20},{20,16},{24,28},{28,24},{1,5},{5... | collective-permute-start | bytes 786440 | tf_op jit(solution)/shard_map/ppermute | solution.py:52
  202.4 27.7 %collective-permute-start.7 = (bf16[128,1024]{1,0:T(8,128)(2,1)}, bf16[128,1024]{1,0:T(8,128)(2,1)S(1)}, u32[]{:S(2)}, u32[]{:S(2)}) collective-permute-start(bf16[128,1024]{1,0:T(8,128)(2,1)} %get-tuple-element.107), channel_id=1, source_target_pairs={{0,8},{4,12},{8,0},{12,4},{16,24},{20,28},{24,16},{28,20},{1,9},{5... | collective-permute-start | bytes 786440 | tf_op jit(solution)/shard_map/ppermute | solution.py:52
  207.2 52.9 %collective-permute-start.8 = (bf16[128,1024]{1,0:T(8,128)(2,1)}, bf16[128,1024]{1,0:T(8,128)(2,1)S(1)}, u32[]{:S(2)}, u32[]{:S(2)}) collective-permute-start(bf16[128,1024]{1,0:T(8,128)(2,1)} %get-tuple-element.108), channel_id=1, source_target_pairs={{0,12},{4,8},{8,4},{12,0},{16,28},{20,24},{24,20},{28,16},{1,13},{... | collective-permute-start | bytes 786440 | tf_op jit(solution)/shard_map/ppermute | solution.py:52
  229.9 30.9 %collective-permute-start.9 = (bf16[128,1024]{1,0:T(8,128)(2,1)}, bf16[128,1024]{1,0:T(8,128)(2,1)S(1)}, u32[]{:S(2)}, u32[]{:S(2)}) collective-permute-start(bf16[128,1024]{1,0:T(8,128)(2,1)} %get-tuple-element.109), channel_id=1, source_target_pairs={{0,16},{4,20},{8,24},{12,28},{16,0},{20,4},{24,8},{28,12},{1,17},{... | collective-permute-start | bytes 786440 | tf_op jit(solution)/shard_map/ppermute | solution.py:52
  230.0 36.7 %collective-permute-start.10 = (bf16[128,1024]{1,0:T(8,128)(2,1)}, bf16[128,1024]{1,0:T(8,128)(2,1)S(1)}, u32[]{:S(2)}, u32[]{:S(2)}) collective-permute-start(bf16[128,1024]{1,0:T(8,128)(2,1)} %get-tuple-element.110), channel_id=1, source_target_pairs={{0,20},{4,16},{8,28},{12,24},{16,4},{20,0},{24,12},{28,8},{1,21},{... | collective-permute-start | bytes 786440 | tf_op jit(solution)/shard_map/ppermute | solution.py:52
  233.8 32.9 %collective-permute-start.11 = (bf16[128,1024]{1,0:T(8,128)(2,1)}, bf16[128,1024]{1,0:T(8,128)(2,1)S(1)}, u32[]{:S(2)}, u32[]{:S(2)}) collective-permute-start(bf16[128,1024]{1,0:T(8,128)(2,1)} %get-tuple-element.111), channel_id=1, source_target_pairs={{0,24},{4,28},{8,16},{12,20},{16,8},{20,12},{24,0},{28,4},{1,25},{... | collective-permute-start | bytes 786440 | tf_op jit(solution)/shard_map/ppermute | solution.py:52
  235.1 31.6 %collective-permute-start.12 = (bf16[128,1024]{1,0:T(8,128)(2,1)}, bf16[128,1024]{1,0:T(8,128)(2,1)S(1)}, u32[]{:S(2)}, u32[]{:S(2)}) collective-permute-start(bf16[128,1024]{1,0:T(8,128)(2,1)} %get-tuple-element.112), channel_id=1, source_target_pairs={{0,28},{4,24},{8,20},{12,16},{16,12},{20,8},{24,4},{28,0},{1,29},{... | collective-permute-start | bytes 786440 | tf_op jit(solution)/shard_map/ppermute | solution.py:52
  309.1 16.6 %collective-permute-start.33 = (bf16[128,1024]{1,0:T(8,128)(2,1)}, bf16[128,1024]{1,0:T(8,128)(2,1)S(1)}, u32[]{:S(2)}, u32[]{:S(2)}) collective-permute-start(bf16[128,1024]{1,0:T(8,128)(2,1)} %get-tuple-element.125), channel_id=1, source_target_pairs={{0,4},{4,0},{8,12},{12,8},{16,20},{20,16},{24,28},{28,24},{1,5},{5... | collective-permute-start | bytes 786440 | tf_op jit(solution)/shard_map/ppermute | solution.py:52
  310.3 28.7 %collective-permute-start.34 = (bf16[128,1024]{1,0:T(8,128)(2,1)}, bf16[128,1024]{1,0:T(8,128)(2,1)S(1)}, u32[]{:S(2)}, u32[]{:S(2)}) collective-permute-start(bf16[128,1024]{1,0:T(8,128)(2,1)} %get-tuple-element.126), channel_id=1, source_target_pairs={{0,8},{4,12},{8,0},{12,4},{16,24},{20,28},{24,16},{28,20},{1,9},{5... | collective-permute-start | bytes 786440 | tf_op jit(solution)/shard_map/ppermute | solution.py:52
  321.8 22.2 %collective-permute-start.35 = (bf16[128,1024]{1,0:T(8,128)(2,1)}, bf16[128,1024]{1,0:T(8,128)(2,1)S(1)}, u32[]{:S(2)}, u32[]{:S(2)}) collective-permute-start(bf16[128,1024]{1,0:T(8,128)(2,1)} %get-tuple-element.127), channel_id=1, source_target_pairs={{0,12},{4,8},{8,4},{12,0},{16,28},{20,24},{24,20},{28,16},{1,13},{... | collective-permute-start | bytes 786440 | tf_op jit(solution)/shard_map/ppermute | solution.py:52
  322.1 21.9 %collective-permute-start.36 = (bf16[128,1024]{1,0:T(8,128)(2,1)}, bf16[128,1024]{1,0:T(8,128)(2,1)S(1)}, u32[]{:S(2)}, u32[]{:S(2)}) collective-permute-start(bf16[128,1024]{1,0:T(8,128)(2,1)} %get-tuple-element.128), channel_id=1, source_target_pairs={{0,16},{4,20},{8,24},{12,28},{16,0},{20,4},{24,8},{28,12},{1,17},{... | collective-permute-start | bytes 786440 | tf_op jit(solution)/shard_map/ppermute | solution.py:52
  324.7 36.4 %collective-permute-start.37 = (bf16[128,1024]{1,0:T(8,128)(2,1)}, bf16[128,1024]{1,0:T(8,128)(2,1)S(1)}, u32[]{:S(2)}, u32[]{:S(2)}) collective-permute-start(bf16[128,1024]{1,0:T(8,128)(2,1)} %get-tuple-element.129), channel_id=1, source_target_pairs={{0,20},{4,16},{8,28},{12,24},{16,4},{20,0},{24,12},{28,8},{1,21},{... | collective-permute-start | bytes 786440 | tf_op jit(solution)/shard_map/ppermute | solution.py:52
  325.6 35.5 %collective-permute-start.38 = (bf16[128,1024]{1,0:T(8,128)(2,1)}, bf16[128,1024]{1,0:T(8,128)(2,1)S(1)}, u32[]{:S(2)}, u32[]{:S(2)}) collective-permute-start(bf16[128,1024]{1,0:T(8,128)(2,1)} %get-tuple-element.130), channel_id=1, source_target_pairs={{0,24},{4,28},{8,16},{12,20},{16,8},{20,12},{24,0},{28,4},{1,25},{... | collective-permute-start | bytes 786440 | tf_op jit(solution)/shard_map/ppermute | solution.py:52
  339.1 22.1 %collective-permute-start.39 = (bf16[128,1024]{1,0:T(8,128)(2,1)}, bf16[128,1024]{1,0:T(8,128)(2,1)S(1)}, u32[]{:S(2)}, u32[]{:S(2)}) collective-permute-start(bf16[128,1024]{1,0:T(8,128)(2,1)} %get-tuple-element.131), channel_id=1, source_target_pairs={{0,28},{4,24},{8,20},{12,16},{16,12},{20,8},{24,4},{28,0},{1,29},{... | collective-permute-start | bytes 786440 | tf_op jit(solution)/shard_map/ppermute | solution.py:52
  374.6 13.9 %collective-permute-start.55 = (bf16[256,1024]{1,0:T(8,128)(2,1)S(1)}, bf16[256,1024]{1,0:T(8,128)(2,1)S(1)}, u32[]{:S(2)}, u32[]{:S(2)}) collective-permute-start(bf16[256,1024]{1,0:T(8,128)(2,1)S(1)} %fusion.33), channel_id=1, source_target_pairs={{0,2},{1,3},{2,0},{3,1},{4,6},{5,7},{6,4},{7,5},{8,10},{9,11},{10,... | collective-permute-start | bytes 1572872 | tf_op jit(solution)/shard_map/ppermute | solution.py:52
  389.0 16.2 %collective-permute-start.62 = (bf16[32,1024]{1,0:T(8,128)(2,1)S(1)}, bf16[32,1024]{1,0:T(8,128)(2,1)S(1)}, u32[]{:S(2)}, u32[]{:S(2)}) collective-permute-start(bf16[32,1024]{1,0:T(8,128)(2,1)S(1)} %get-tuple-element.181), channel_id=1, source_target_pairs={{0,28},{4,24},{8,20},{12,16},{16,12},{20,8},{24,4},{28,0},{1,29},{... | collective-permute-start | bytes 196616 | tf_op jit(solution)/shard_map/ppermute | solution.py:52
  391.5 14.6 %collective-permute-start.61 = (bf16[32,1024]{1,0:T(8,128)(2,1)S(1)}, bf16[32,1024]{1,0:T(8,128)(2,1)S(1)}, u32[]{:S(2)}, u32[]{:S(2)}) collective-permute-start(bf16[32,1024]{1,0:T(8,128)(2,1)S(1)} %get-tuple-element.182), channel_id=1, source_target_pairs={{0,24},{4,28},{8,16},{12,20},{16,8},{20,12},{24,0},{28,4},{1,25},{... | collective-permute-start | bytes 196616 | tf_op jit(solution)/shard_map/ppermute | solution.py:52
  393.2 15.8 %collective-permute-start.60 = (bf16[32,1024]{1,0:T(8,128)(2,1)S(1)}, bf16[32,1024]{1,0:T(8,128)(2,1)S(1)}, u32[]{:S(2)}, u32[]{:S(2)}) collective-permute-start(bf16[32,1024]{1,0:T(8,128)(2,1)S(1)} %get-tuple-element.183), channel_id=1, source_target_pairs={{0,20},{4,16},{8,28},{12,24},{16,4},{20,0},{24,12},{28,8},{1,21},{... | collective-permute-start | bytes 196616 | tf_op jit(solution)/shard_map/ppermute | solution.py:52
  411.1 299.8 %all-gather.5.cloned.1.call-start = ((), (), s32[]{:S(2)}) async-start(), calls=%async_computation | async-start | bytes 6488064 | tf_op jit(solution)/shard_map/all_gather | solution.py:708
  412.7 12.9 %collective-permute-start.42 = (bf16[512,256]{1,0:T(8,128)(2,1)S(1)}, bf16[512,256]{1,0:T(8,128)(2,1)S(1)}, u32[]{:S(2)}, u32[]{:S(2)}) collective-permute-start(bf16[512,256]{1,0:T(8,128)(2,1)S(1)} %copy-done.64), channel_id=1, source_target_pairs={{0,3},{1,2},{2,1},{3,0},{4,7},{5,6},{6,5},{7,4},{8,11},{9,10},{10,... | collective-permute-start | bytes 786440 | tf_op jit(solution)/shard_map/ppermute | solution.py:52
  453.4 13.2 %collective-permute-start.52 = (bf16[128,768]{1,0:T(8,128)(2,1)}, bf16[128,768]{1,0:T(8,128)(2,1)S(1)}, u32[]{:S(2)}, u32[]{:S(2)}) collective-permute-start(bf16[128,768]{1,0:T(8,128)(2,1)} %get-tuple-element.159), channel_id=1, source_target_pairs={{0,28},{4,24},{8,20},{12,16},{16,12},{20,8},{24,4},{28,0},{1,29},{... | collective-permute-start | bytes 589832 | tf_op jit(solution)/shard_map/ppermute | solution.py:52
  455.8 30.4 %collective-permute-start.51 = (bf16[128,768]{1,0:T(8,128)(2,1)}, bf16[128,768]{1,0:T(8,128)(2,1)S(1)}, u32[]{:S(2)}, u32[]{:S(2)}) collective-permute-start(bf16[128,768]{1,0:T(8,128)(2,1)} %get-tuple-element.158), channel_id=1, source_target_pairs={{0,24},{4,28},{8,16},{12,20},{16,8},{20,12},{24,0},{28,4},{1,25},{... | collective-permute-start | bytes 589832 | tf_op jit(solution)/shard_map/ppermute | solution.py:52
  457.4 35.9 %collective-permute-start.50 = (bf16[128,768]{1,0:T(8,128)(2,1)}, bf16[128,768]{1,0:T(8,128)(2,1)S(1)}, u32[]{:S(2)}, u32[]{:S(2)}) collective-permute-start(bf16[128,768]{1,0:T(8,128)(2,1)} %get-tuple-element.157), channel_id=1, source_target_pairs={{0,20},{4,16},{8,28},{12,24},{16,4},{20,0},{24,12},{28,8},{1,21},{... | collective-permute-start | bytes 589832 | tf_op jit(solution)/shard_map/ppermute | solution.py:52
  458.3 39.4 %collective-permute-start.49 = (bf16[128,768]{1,0:T(8,128)(2,1)}, bf16[128,768]{1,0:T(8,128)(2,1)S(1)}, u32[]{:S(2)}, u32[]{:S(2)}) collective-permute-start(bf16[128,768]{1,0:T(8,128)(2,1)} %get-tuple-element.156), channel_id=1, source_target_pairs={{0,16},{4,20},{8,24},{12,28},{16,0},{20,4},{24,8},{28,12},{1,17},{... | collective-permute-start | bytes 589832 | tf_op jit(solution)/shard_map/ppermute | solution.py:52
  461.1 36.6 %collective-permute-start.48 = (bf16[128,768]{1,0:T(8,128)(2,1)}, bf16[128,768]{1,0:T(8,128)(2,1)S(1)}, u32[]{:S(2)}, u32[]{:S(2)}) collective-permute-start(bf16[128,768]{1,0:T(8,128)(2,1)} %get-tuple-element.155), channel_id=1, source_target_pairs={{0,12},{4,8},{8,4},{12,0},{16,28},{20,24},{24,20},{28,16},{1,13},{... | collective-permute-start | bytes 589832 | tf_op jit(solution)/shard_map/ppermute | solution.py:52
  466.6 32.8 %collective-permute-start.47 = (bf16[128,768]{1,0:T(8,128)(2,1)}, bf16[128,768]{1,0:T(8,128)(2,1)S(1)}, u32[]{:S(2)}, u32[]{:S(2)}) collective-permute-start(bf16[128,768]{1,0:T(8,128)(2,1)} %get-tuple-element.154), channel_id=1, source_target_pairs={{0,8},{4,12},{8,0},{12,4},{16,24},{20,28},{24,16},{28,20},{1,9},{5... | collective-permute-start | bytes 589832 | tf_op jit(solution)/shard_map/ppermute | solution.py:52
  486.2 13.2 %collective-permute-start.46 = (bf16[128,768]{1,0:T(8,128)(2,1)}, bf16[128,768]{1,0:T(8,128)(2,1)S(1)}, u32[]{:S(2)}, u32[]{:S(2)}) collective-permute-start(bf16[128,768]{1,0:T(8,128)(2,1)} %get-tuple-element.153), channel_id=1, source_target_pairs={{0,4},{4,0},{8,12},{12,8},{16,20},{20,16},{24,28},{28,24},{1,5},{5... | collective-permute-start | bytes 589832 | tf_op jit(solution)/shard_map/ppermute | solution.py:52
  512.9 19.9 %collective-permute-start.44 = (bf16[512,1024]{1,0:T(8,128)(2,1)}, bf16[512,1024]{1,0:T(8,128)(2,1)S(1)}, u32[]{:S(2)}, u32[]{:S(2)}) collective-permute-start(bf16[512,1024]{1,0:T(8,128)(2,1)} %get-tuple-element.146), channel_id=1, source_target_pairs={{0,1},{1,0},{2,3},{3,2},{4,5},{5,4},{6,7},{7,6},{8,9},{9,8},{10,11... | collective-permute-start | bytes 3145736 | tf_op jit(solution)/shard_map/ppermute | solution.py:52
  532.3 55.3 %collective-permute-start.69 = (bf16[1024,1024]{1,0:T(8,128)(2,1)}, bf16[1024,1024]{1,0:T(8,128)(2,1)}, u32[]{:S(2)}, u32[]{:S(2)}) collective-permute-start(bf16[1024,1024]{1,0:T(8,128)(2,1)} %fusion.19), channel_id=1, source_target_pairs={{0,1},{1,0},{2,3},{3,2},{4,5},{5,4},{6,7},{7,6},{8,9},{9,8},{10,11... | collective-permute-start | bytes 6291464 | tf_op jit(solution)/shard_map/ppermute | solution.py:52
  532.8 12.9 %collective-permute-start.43 = (bf16[512,1024]{1,0:T(8,128)(2,1)S(1)}, bf16[512,1024]{1,0:T(8,128)(2,1)S(1)}, u32[]{:S(2)}, u32[]{:S(2)}) collective-permute-start(bf16[512,1024]{1,0:T(8,128)(2,1)S(1)} %copy-done.63), channel_id=1, source_target_pairs={{0,1},{1,0},{2,3},{3,2},{4,5},{5,4},{6,7},{7,6},{8,9},{9,8},{10,11... | collective-permute-start | bytes 3145736 | tf_op jit(solution)/shard_map/ppermute | solution.py:52
  533.2 36.6 %collective-permute-start.45 = (bf16[512,1024]{1,0:T(8,128)(2,1)S(1)}, bf16[512,1024]{1,0:T(8,128)(2,1)S(1)}, u32[]{:S(2)}, u32[]{:S(2)}) collective-permute-start(bf16[512,1024]{1,0:T(8,128)(2,1)S(1)} %add_convert_fusion.2), channel_id=1, source_target_pairs={{0,2},{1,3},{2,0},{3,1},{4,6},{5,7},{6,4},{7,5},{8,10},{9,11},{10,... | collective-permute-start | bytes 3145736 | tf_op jit(solution)/shard_map/ppermute | solution.py:52
  540.1 68.5 %collective-permute-start.72 = (bf16[1024,1024]{1,0:T(8,128)(2,1)}, bf16[1024,1024]{1,0:T(8,128)(2,1)}, u32[]{:S(2)}, u32[]{:S(2)}) collective-permute-start(bf16[1024,1024]{1,0:T(8,128)(2,1)} %fusion.25), channel_id=1, source_target_pairs={{0,1},{1,0},{2,3},{3,2},{4,5},{5,4},{6,7},{7,6},{8,9},{9,8},{10,11... | collective-permute-start | bytes 6291464 | tf_op jit(solution)/shard_map/ppermute | solution.py:52
  586.0 11.6 %collective-permute-start.26 = (bf16[128,1024]{1,0:T(8,128)(2,1)S(1)}, bf16[128,1024]{1,0:T(8,128)(2,1)S(1)}, u32[]{:S(2)}, u32[]{:S(2)}) collective-permute-start(bf16[128,1024]{1,0:T(8,128)(2,1)S(1)} %get-tuple-element.178), channel_id=1, source_target_pairs={{0,4},{4,0},{8,12},{12,8},{16,20},{20,16},{24,28},{28,24},{1,5},{5... | collective-permute-start | bytes 786440 | tf_op jit(solution)/shard_map/ppermute | solution.py:52
  587.5 15.6 %collective-permute-start.27 = (bf16[128,1024]{1,0:T(8,128)(2,1)S(1)}, bf16[128,1024]{1,0:T(8,128)(2,1)S(1)}, u32[]{:S(2)}, u32[]{:S(2)}) collective-permute-start(bf16[128,1024]{1,0:T(8,128)(2,1)S(1)} %get-tuple-element.177), channel_id=1, source_target_pairs={{0,8},{4,12},{8,0},{12,4},{16,24},{20,28},{24,16},{28,20},{1,9},{5... | collective-permute-start | bytes 786440 | tf_op jit(solution)/shard_map/ppermute | solution.py:52
  587.6 20.0 %collective-permute-start.28 = (bf16[128,1024]{1,0:T(8,128)(2,1)S(1)}, bf16[128,1024]{1,0:T(8,128)(2,1)S(1)}, u32[]{:S(2)}, u32[]{:S(2)}) collective-permute-start(bf16[128,1024]{1,0:T(8,128)(2,1)S(1)} %get-tuple-element.176), channel_id=1, source_target_pairs={{0,12},{4,8},{8,4},{12,0},{16,28},{20,24},{24,20},{28,16},{1,13},{... | collective-permute-start | bytes 786440 | tf_op jit(solution)/shard_map/ppermute | solution.py:52
  589.5 18.1 %collective-permute-start.29 = (bf16[128,1024]{1,0:T(8,128)(2,1)S(1)}, bf16[128,1024]{1,0:T(8,128)(2,1)S(1)}, u32[]{:S(2)}, u32[]{:S(2)}) collective-permute-start(bf16[128,1024]{1,0:T(8,128)(2,1)S(1)} %get-tuple-element.175), channel_id=1, source_target_pairs={{0,16},{4,20},{8,24},{12,28},{16,0},{20,4},{24,8},{28,12},{1,17},{... | collective-permute-start | bytes 786440 | tf_op jit(solution)/shard_map/ppermute | solution.py:52
  597.6 27.1 %collective-permute-start.30 = (bf16[128,1024]{1,0:T(8,128)(2,1)S(1)}, bf16[128,1024]{1,0:T(8,128)(2,1)S(1)}, u32[]{:S(2)}, u32[]{:S(2)}) collective-permute-start(bf16[128,1024]{1,0:T(8,128)(2,1)S(1)} %get-tuple-element.174), channel_id=1, source_target_pairs={{0,20},{4,16},{8,28},{12,24},{16,4},{20,0},{24,12},{28,8},{1,21},{... | collective-permute-start | bytes 786440 | tf_op jit(solution)/shard_map/ppermute | solution.py:52
  603.1 21.9 %collective-permute-start.31 = (bf16[128,1024]{1,0:T(8,128)(2,1)S(1)}, bf16[128,1024]{1,0:T(8,128)(2,1)S(1)}, u32[]{:S(2)}, u32[]{:S(2)}) collective-permute-start(bf16[128,1024]{1,0:T(8,128)(2,1)S(1)} %get-tuple-element.173), channel_id=1, source_target_pairs={{0,24},{4,28},{8,16},{12,20},{16,8},{20,12},{24,0},{28,4},{1,25},{... | collective-permute-start | bytes 786440 | tf_op jit(solution)/shard_map/ppermute | solution.py:52
  607.6 48.2 %collective-permute-start.68 = (bf16[1024,1024]{1,0:T(8,128)(2,1)}, bf16[1024,1024]{1,0:T(8,128)(2,1)S(1)}, u32[]{:S(2)}, u32[]{:S(2)}) collective-permute-start(bf16[1024,1024]{1,0:T(8,128)(2,1)} %fusion.16), channel_id=1, source_target_pairs={{0,1},{1,0},{2,3},{3,2},{4,5},{5,4},{6,7},{7,6},{8,9},{9,8},{10,11... | collective-permute-start | bytes 6291464 | tf_op jit(solution)/shard_map/ppermute | solution.py:52
  607.6 48.8 %collective-permute-start.70 = (bf16[1024,1024]{1,0:T(8,128)(2,1)}, bf16[1024,1024]{1,0:T(8,128)(2,1)}, u32[]{:S(2)}, u32[]{:S(2)}) collective-permute-start(bf16[1024,1024]{1,0:T(8,128)(2,1)} %add_convert_fusion.1), channel_id=1, source_target_pairs={{0,2},{1,3},{2,0},{3,1},{4,6},{5,7},{6,4},{7,5},{8,10},{9,11},{10,... | collective-permute-start | bytes 6291464 | tf_op jit(solution)/shard_map/ppermute | solution.py:52
  608.6 16.1 %collective-permute-start.65 = (f32[2,1024]{1,0:T(2,128)S(1)}, f32[2,1024]{1,0:T(2,128)S(1)}, u32[]{:S(2)}, u32[]{:S(2)}) collective-permute-start(f32[2,1024]{1,0:T(2,128)S(1)} %fusion.55), channel_id=1, source_target_pairs={{0,4},{4,0},{8,12},{12,8},{16,20},{20,16},{24,28},{28,24},{1,5},{5... | collective-permute-start | bytes 24584 | tf_op jit(solution)/shard_map/ppermute | solution.py:52
  624.7 37.7 %collective-permute-start.71 = (bf16[1024,1024]{1,0:T(8,128)(2,1)}, bf16[1024,1024]{1,0:T(8,128)(2,1)}, u32[]{:S(2)}, u32[]{:S(2)}) collective-permute-start(bf16[1024,1024]{1,0:T(8,128)(2,1)} %fusion.22), channel_id=1, source_target_pairs={{0,1},{1,0},{2,3},{3,2},{4,5},{5,4},{6,7},{7,6},{8,9},{9,8},{10,11... | collective-permute-start | bytes 6291464 | tf_op jit(solution)/shard_map/ppermute | solution.py:52
  624.7 76.2 %collective-permute-start.73 = (bf16[1024,1024]{1,0:T(8,128)(2,1)}, bf16[1024,1024]{1,0:T(8,128)(2,1)}, u32[]{:S(2)}, u32[]{:S(2)}) collective-permute-start(bf16[1024,1024]{1,0:T(8,128)(2,1)} %add_convert_fusion), channel_id=1, source_target_pairs={{0,2},{1,3},{2,0},{3,1},{4,6},{5,7},{6,4},{7,5},{8,10},{9,11},{10,... | collective-permute-start | bytes 6291464 | tf_op jit(solution)/shard_map/ppermute | solution.py:52
  625.1 9.8 %collective-permute-start.66 = (f32[2,1024]{1,0:T(2,128)S(1)}, f32[2,1024]{1,0:T(2,128)S(1)}, u32[]{:S(2)}, u32[]{:S(2)}) collective-permute-start(f32[2,1024]{1,0:T(2,128)S(1)} %add.139), channel_id=1, source_target_pairs={{0,8},{4,12},{8,0},{12,4},{16,24},{20,28},{24,16},{28,20},{1,9},{5... | collective-permute-start | bytes 24584 | tf_op jit(solution)/shard_map/ppermute | solution.py:52
  634.9 10.2 %collective-permute-start.32 = (bf16[128,1024]{1,0:T(8,128)(2,1)S(1)}, bf16[128,1024]{1,0:T(8,128)(2,1)S(1)}, u32[]{:S(2)}, u32[]{:S(2)}) collective-permute-start(bf16[128,1024]{1,0:T(8,128)(2,1)S(1)} %get-tuple-element.172), channel_id=1, source_target_pairs={{0,28},{4,24},{8,20},{12,16},{16,12},{20,8},{24,4},{28,0},{1,29},{... | collective-permute-start | bytes 786440 | tf_op jit(solution)/shard_map/ppermute | solution.py:52
  645.1 10.2 %collective-permute-start.67 = (f32[2,1024]{1,0:T(2,128)S(1)}, f32[2,1024]{1,0:T(2,128)S(1)}, u32[]{:S(2)}, u32[]{:S(2)}) collective-permute-start(f32[2,1024]{1,0:T(2,128)S(1)} %add.140), channel_id=1, source_target_pairs={{0,16},{4,20},{8,24},{12,28},{16,0},{20,4},{24,8},{28,12},{1,17},{... | collective-permute-start | bytes 24584 | tf_op jit(solution)/shard_map/ppermute | solution.py:52
  (86 other events, 1023.0 us)
Sparse Core Ops, SparseCore 0:
  411.2 71.1 all-gather.6
  501.4 77.7 all-gather.4
